TPU v7x, 256 devices: a whole 4x4x8 slice. The times are simulated.
256 devices in a mesh: gx: 8 (over z), gy: 8 (over x, core), gz: 4 (over y).
Axes of the slice: x: 4, y: 4, z: 8, core: 2. Of those that a mesh axis runs over, the one named last changes fastest.
Arguments:
- adjoint: bfloat16 [4, 16384, 512], P(None, ('gx', 'gy', 'gz')), may hold values from -6 to 6
- load: bfloat16 [4, 16384, 512], P(None, ('gx', 'gy', 'gz')), may hold values from -4 to 4
- displace: bfloat16 [3, 16384, 512], P(None, ('gx', 'gy', 'gz')), may hold values from -4 to 4
- damage: bfloat16 [16384, 512], P(('gx', 'gy', 'gz')), may hold values from 0 to 0.8984375
- history: bfloat16 [16384, 512], P(('gx', 'gy', 'gz')), may hold values from 0 to 20
- frozen: int32 [16384], P(('gx', 'gy', 'gz')), may hold values 0 or 1
- order: int32 [256, 64], P(('gx', 'gy', 'gz')), may hold values from 0 to 63, each once within a row
Outputs:
- residual: float32 [4, 16384, 512], P(None, ('gx', 'gy', 'gz'))
Inputs may be any that keep to these rules, and one draw needn't show every extreme that they name: `order`: each device's row of 64 entries holds every local place once.
All inputs are finite; a program needn't handle non-finite values. No bound on the sum of `frozen` on one device may be relied on, other than what follows from the above.
Results may differ from a plain program's by a relative error of at most 0.00035.
Values sent between devices are 32-bit elements; how exact they have to be, the bound alone decides.
A program may use at most 64 MiB of HBM per device.

v0:
```python
import jax
import jax.numpy as jnp
import ml_dtypes
import numpy as np
from jax import lax
from jax.experimental import pallas as pl
from jax.experimental.pallas import tpu as pltpu
from jax.sharding import PartitionSpec as P

F32 = jnp.float32
BF16 = jnp.bfloat16
MESH = pl.DeviceIdType.MESH

lame_lambda = 0.15
lame_mu = 0.1
gc_length = 0.3
gc_inverse = 40.0
residual_stiff = 0.001
relaxation = 0.5
gll_points = (
    -1.0,
    -0.8717401485096066,
    -0.5917001814331423,
    -0.2092992179024789,
    0.2092992179024789,
    0.5917001814331423,
    0.8717401485096066,
    1.0,
)

DIRS = [
    (dx, dy, dz)
    for dx in (-1, 0, 1)
    for dy in (-1, 0, 1)
    for dz in (-1, 0, 1)
    if (dx, dy, dz) != (0, 0, 0)
]
X_DIRS = [d for d in DIRS if d[1] == 0 and d[2] == 0]
Y_DIRS = [d for d in DIRS if d[0] == 0 and d[1] != 0 and d[2] == 0]
XY_DIRS = [d for d in DIRS if d[0] != 0 and d[1] != 0 and d[2] == 0]
Z_DIRS = [d for d in DIRS if d[2] != 0]
SEND_ORDER = X_DIRS + Y_DIRS + XY_DIRS + Z_DIRS


def legendre_at(points, degree):
    values = []
    for point in points:
        previous = 1.0
        current = point
        for level in range(1, degree):
            following = ((2 * level + 1) * point * current - level * previous) / (level + 1)
            previous = current
            current = following
        values.append(current)
    return values


def gll_tables():
    degree = 7
    points = list(gll_points)
    legendre_vals = legendre_at(points, degree)
    weights = [2.0 / (degree * (degree + 1) * entry * entry) for entry in legendre_vals]
    derivative = []
    for row_index in range(degree + 1):
        row_vals = []
        for col_index in range(degree + 1):
            if row_index != col_index:
                row_vals.append(
                    legendre_vals[row_index]
                    / (legendre_vals[col_index] * (points[row_index] - points[col_index]))
                )
            else:
                row_vals.append(0.0)
        derivative.append(row_vals)
    derivative[0][0] = -degree * (degree + 1) / 4.0
    derivative[degree][degree] = degree * (degree + 1) / 4.0
    return (np.array(weights), np.array(derivative))


def split_np(matrix):
    high = matrix.astype(np.float32).astype(ml_dtypes.bfloat16)
    low = (matrix - high.astype(np.float64)).astype(np.float32).astype(ml_dtypes.bfloat16)
    return high, low


def even_odd_rows(matrix):
    even = (matrix + matrix[:, ::-1]) / 2
    odd = (matrix - matrix[:, ::-1]) / 2
    rows = []
    for part in (even, odd):
        for a in range(2):
            for b in range(2):
                same = [part[2 * a + h, 2 * b + h] for h in range(2)]
                cross = [part[2 * a + h, 2 * b + 1 - h] for h in range(2)]
                rows.append(np.repeat(same, 64))
                rows.append(np.repeat(cross, 64))
    return rows


def constants():
    weights, derivative = gll_tables()
    eye = np.eye
    forward_y = np.kron(eye(2), np.kron(derivative.T, eye(8)))
    forward_z = np.kron(eye(16), derivative.T)
    back_y = np.kron(eye(2), np.kron(derivative, eye(8)))
    back_z = np.kron(eye(16), derivative)
    f_high, f_low = split_np(np.concatenate([forward_y, forward_z], axis=1))
    forward = np.concatenate([f_high, f_high, f_low], axis=0)
    b_high, b_low = split_np(np.concatenate([back_y, back_z], axis=0))
    back = np.concatenate([b_high, b_low], axis=1)
    brick = (weights[:, None, None] * weights[None, :, None] * weights[None, None, :]).reshape(4, 128)
    rows = even_odd_rows(derivative) + even_odd_rows(derivative.T) + list(brick)
    rows = np.stack(rows + [np.zeros(128)] * 4).astype(np.float32)
    return forward, back, rows


def lane_roll(value, shift):
    shift = shift % 128
    if shift == 0:
        return value
    flat = value.reshape(-1, 128)
    return pltpu.roll(flat, shift, 1).reshape(value.shape)


def split(value):
    high = value.astype(BF16)
    low = (value - high.astype(F32)).astype(BF16)
    return high, low


def x_derivative(tiles, table, base):
    def row(index):
        return table[base + index : base + index + 1, :]

    r2 = lane_roll(tiles[2], 64)
    r3 = lane_roll(tiles[3], 64)
    even = [tiles[0] + r3, tiles[1] + r2]
    odd = [tiles[0] - r3, tiles[1] - r2]
    even_r = [lane_roll(v, 64) for v in even]
    odd_r = [lane_roll(v, 64) for v in odd]
    out = [None] * 4
    for a in range(2):
        parts = []
        for start, own, crossed in ((0, even, even_r), (8, odd, odd_r)):
            k = start + 4 * a
            parts.append(
                row(k) * own[0] + row(k + 1) * crossed[0] + row(k + 2) * own[1] + row(k + 3) * crossed[1]
            )
        out[a] = parts[1] + parts[0]
        out[3 - a] = lane_roll(parts[1] - parts[0], 64)
    return out


def kernel(
    adjoint_h,
    load_h,
    displace_h,
    damage_h,
    history_h,
    frozen_h,
    order_h,
    forward_h,
    back_h,
    table_h,
    out_ref,
    adjoint_b,
    load_b,
    displace_b,
    damage_b,
    history_b,
    frozen_b,
    order_b,
    forward,
    back,
    table,
    value,
    load,
    summed,
    state,
    keep,
    xs,
    ys,
    zs,
    xr,
    yr,
    xyr,
    zr,
    in_sem,
    send_sem,
    recv_sem,
):
    px, py, pz = (lax.axis_index("gx"), lax.axis_index("gy"), lax.axis_index("gz"))
    sizes = (lax.axis_size("gx"), lax.axis_size("gy"), lax.axis_size("gz"))

    pairs = (
        (order_h, order_b),
        (adjoint_h, adjoint_b),
        (displace_h, displace_b),
        (damage_h, damage_b),
        (history_h, history_b),
        (frozen_h, frozen_b),
        (forward_h, forward),
        (table_h, table),
        (load_h, load_b),
        (back_h, back),
    )
    copies = [pltpu.make_async_copy(src, dst, in_sem.at[n]) for n, (src, dst) in enumerate(pairs)]
    for copy in copies:
        copy.start()

    along = [
        {
            -1: lax.rem(p + n - 1, n),
            0: p,
            1: lax.rem(p + 1, n),
        }
        for p, n in zip((px, py, pz), sizes)
    ]

    def target(d):
        return tuple(along[axis][d[axis]] for axis in range(3))

    barrier = pltpu.get_barrier_semaphore()
    for d in DIRS:
        pl.semaphore_signal(barrier, inc=1, device_id=target(d), device_id_type=MESH)

    present = [
        {
            -1: (p > 0).astype(F32),
            1: (p < n - 1).astype(F32),
        }
        for p, n in zip((px, py, pz), sizes)
    ]

    lane = lax.broadcasted_iota(jnp.int32, (8, 128), 1)
    sub = lax.broadcasted_iota(jnp.int32, (8, 128), 0)
    lane_k = lane % 8
    lane_j = (lane // 8) % 8
    lane_h = lane // 64

    def fmask(condition):
        return jnp.where(condition, 1.0, 0.0).astype(F32)

    k_end = {-1: fmask(lane_k == 0), 1: fmask(lane_k == 7)}
    j_end = {-1: fmask(lane_j == 0), 1: fmask(lane_j == 7)}
    h_end = {-1: fmask(lane_h == 0), 1: fmask(lane_h == 1)}

    copies[0].wait()
    row_id = lax.broadcasted_iota(jnp.int32, (64, 64), 0)
    place = (row_id // 16) * 16 + 2 * (row_id % 8) + (row_id // 8) % 2
    chosen = fmask(place == order_b[...])
    pick = chosen.astype(BF16)
    unpick = chosen.T.astype(BF16)

    def placed(stored):
        return jnp.dot(pick, stored, preferred_element_type=F32)

    def to_rows(ref, target_ref):
        for f in range(4):
            rows = placed(ref[f])
            for a in range(4):
                target_ref[a, f * 64 : f * 64 + 64, :] = rows[:, a * 128 : a * 128 + 128]

    def sum_local():
        z_up = k_end[1] * fmask(sub < 7)
        z_down = k_end[-1] * fmask(sub > 0)
        for f in range(4):
            block = summed[:, f * 64 : f * 64 + 64, :].reshape(16, 2, 8, 128)
            x0, x1 = block[:, 0], block[:, 1]
            y0 = x0 + k_end[1] * lane_roll(x1, 7) + z_down * pltpu.roll(lane_roll(x1, -7), 1, 1)
            y1 = x1 + k_end[-1] * lane_roll(x0, -7) + z_up * pltpu.roll(lane_roll(x0, 7), 7, 1)
            both = jnp.stack([y0, y1], axis=1).reshape(4, 4, 16, 128)
            upper = j_end[1] * lane_roll(both[:, 1:], 56).reshape(4, 3, 2, 8, 128)
            lower = j_end[-1] * lane_roll(both[:, :3], -56).reshape(4, 3, 2, 8, 128)
            upper = upper.reshape(4, 3, 16, 128)
            lower = lower.reshape(4, 3, 16, 128)
            base = f * 64
            summed[:, base : base + 16, :] = both[:, 0] + upper[:, 0]
            summed[:, base + 16 : base + 32, :] = both[:, 1] + upper[:, 1] + lower[:, 0]
            summed[:, base + 32 : base + 48, :] = both[:, 2] + upper[:, 2] + lower[:, 1]
            summed[:, base + 48 : base + 64, :] = both[:, 3] + lower[:, 2]

    low_half = lax.broadcasted_iota(jnp.int32, (64, 128), 1) < 64
    wide_j = (lax.broadcasted_iota(jnp.int32, (16, 128), 1) // 8) % 8

    def pack(r):
        for p in range(2):
            first, second = 2 * p * 64, (2 * p + 1) * 64
            xs[r, 0, p] = jnp.where(
                low_half,
                summed[0, first : first + 64, :],
                lane_roll(summed[0, second : second + 64, :], 64),
            )
            xs[r, 1, p] = jnp.where(
                low_half,
                lane_roll(summed[3, first : first + 64, :], 64),
                summed[3, second : second + 64, :],
            )
        for n, (row, j) in enumerate(((0, 0), (48, 7))):
            for g in range(2):
                packed = jnp.zeros((16, 128), F32)
                for slot in range(8):
                    f, a = slot // 2, 2 * g + slot % 2
                    piece = lane_roll(summed[a, f * 64 + row : f * 64 + row + 16, :], 8 * (slot - j))
                    packed = jnp.where(wide_j == slot, piece, packed)
                ys[r, n, g] = packed
        for n, (row, k) in enumerate(((0, 0), (15, 7))):
            packed = jnp.zeros((8, 128), F32)
            for slot in range(8):
                a, half = slot // 2, slot % 2
                piece = summed[a, pl.ds(half * 128 + row, 8, stride=16), :]
                packed = jnp.where(lane_k == slot, lane_roll(piece, slot - k), packed)
            zs[r, n] = packed

    def message(r, d):
        n = DIRS.index(d)
        dx, dy, dz = d
        if d in X_DIRS:
            src, dst = xs.at[r, (dx + 1) // 2], xr.at[r, (dx + 1) // 2]
        elif d in Y_DIRS:
            src, dst = ys.at[r, (dy + 1) // 2], yr.at[r, (dy + 1) // 2]
        elif d in XY_DIRS:
            src, dst = ys.at[r, (dy + 1) // 2, (dx + 1) // 2], xyr.at[r, XY_DIRS.index(d)]
        else:
            src, dst = zs.at[r, (dz + 1) // 2], zr.at[r, Z_DIRS.index(d)]
        return pltpu.make_async_remote_copy(
            src_ref=src,
            dst_ref=dst,
            send_sem=send_sem.at[r, n],
            recv_sem=recv_sem.at[r, n],
            device_id=target(d),
            device_id_type=MESH,
        )

    def send(r):
        messages = {d: message(r, d) for d in SEND_ORDER}
        for d in SEND_ORDER:
            messages[d].start()
        return messages

    def receive(r, messages):
        for d in X_DIRS:
            messages[d].wait_recv()
            n = (d[0] + 1) // 2
            side = -d[0]
            a = 0 if side < 0 else 3
            weight = present[0][side]
            for f in range(4):
                face = xr[r, n, f // 2]
                if (f % 2 == 1) == (side < 0):
                    face = lane_roll(face, 64)
                mine = low_half if side < 0 else jnp.logical_not(low_half)
                rows = slice(f * 64, f * 64 + 64)
                summed[a, rows, :] += jnp.where(mine, face * weight, 0.0)
        for d in Y_DIRS:
            messages[d].wait_recv()
            dy = d[1]
            side = -dy
            faces = [yr[r, (dy + 1) // 2, g] for g in range(2)]
            for dx in (-1, 1):
                e = (dx, dy, 0)
                messages[e].wait_recv()
                edge = lane_roll(xyr[r, XY_DIRS.index(e)], -72 * dx).reshape(2, 8, 128)
                wanted = fmask(lane_j % 2 == (0 if dx > 0 else 1)) * h_end[-dx] * present[0][-dx]
                g = 0 if dx > 0 else 1
                faces[g] = faces[g] + (edge * wanted).reshape(16, 128)
            row, j = (0, 0) if side < 0 else (48, 7)
            wanted = j_end[side] * present[1][side]
            for f in range(4):
                for a in range(4):
                    slot = f * 2 + a % 2
                    piece = lane_roll(faces[a // 2], 8 * (j - slot)).reshape(2, 8, 128) * wanted
                    rows = slice(f * 64 + row, f * 64 + row + 16)
                    summed[a, rows, :] += piece.reshape(16, 128)
        for dz in (-1, 1):
            side = -dz
            face = None
            for d in Z_DIRS:
                if d[2] != dz:
                    continue
                messages[d].wait_recv()
                part = zr[r, Z_DIRS.index(d)]
                dx, dy, _ = d
                wanted = None
                if dx != 0:
                    slots = (lane_k < 2) if dx > 0 else (lane_k >= 6)
                    wanted = h_end[-dx] * fmask(slots) * present[0][-dx]
                if dy != 0:
                    mine = j_end[-dy] * fmask(sub % 4 == (0 if dy > 0 else 3)) * present[1][-dy]
                    wanted = mine if wanted is None else wanted * mine
                    part = pltpu.roll(part, (-3 * dy) % 8, 0)
                part = lane_roll(part, -70 * dx - 56 * dy)
                if wanted is not None:
                    part = part * wanted
                face = part if face is None else face + part
            row, k = (0, 0) if side < 0 else (15, 7)
            wanted = k_end[side] * present[2][side]
            for slot in range(8):
                a, half = slot // 2, slot % 2
                where = pl.ds(half * 128 + row, 8, stride=16)
                summed[a, where, :] = summed[a, where, :] + lane_roll(face, k - slot) * wanted

    def finish(messages):
        for d in SEND_ORDER:
            messages[d].wait_send()

    def w_rows():
        return table[32:36, :].reshape(4, 1, 128)

    def state_terms():
        for e in range(4):
            rows = slice(16 * e, 16 * e + 16)
            moved = [
                jnp.stack([value[a, f * 64 + 16 * e : f * 64 + 16 * e + 16, :] for a in range(4)])
                for f in range(3)
            ]
            stacked = jnp.stack(moved).reshape(192, 128).astype(BF16)
            both = jnp.concatenate([stacked, stacked], axis=1)
            yz = jnp.dot(both, forward[128:384, :], preferred_element_type=F32)
            gy = yz[:, :128].reshape(3, 4, 16, 128)
            gz = yz[:, 128:].reshape(3, 4, 16, 128)
            gx = [
                jnp.stack(x_derivative([moved[f][a] for a in range(4)], table, 0))
                for f in range(3)
            ]
            shear = [gy[0] + gx[1], gz[0] + gx[2], gz[1] + gy[2]]
            normal = [gx[0], gy[1], gz[2]]
            trace_sum = normal[0] + normal[1] + normal[2]
            stress = [lame_lambda * trace_sum + 2.0 * lame_mu * n for n in normal]
            stress += [lame_mu * s for s in shear]
            energy = stress[0] * normal[0] + stress[1] * normal[1] + stress[2] * normal[2]
            energy = 0.5 * (energy + stress[3] * shear[0] + stress[4] * shear[1] + stress[5] * shear[2])
            damage = keep[0, :, rows, :]
            history = keep[1, :, rows, :]
            loading = keep[2, 0, rows, :][None]
            driving = (1.0 - loading) * history + loading * energy
            intact = 1.0 - damage
            brick = w_rows()
            slope = -2.0 * intact * brick
            for n in range(6):
                state[n, :, rows, :] = slope * stress[n]
            state[6, :, rows, :] = lame_mu * brick * (intact * intact + residual_stiff)
            state[7, :, rows, :] = brick * (gc_inverse + 2.0 * driving)

    def apply_transposed():
        for e in range(4):
            rows = slice(16 * e, 16 * e + 16)
            field = [value[:, f * 64 + 16 * e : f * 64 + 16 * e + 16, :] for f in range(4)]
            high, low = split(jnp.stack(field).reshape(256, 128))
            three = jnp.concatenate([high, low, high], axis=1)
            yz = jnp.dot(three, forward[...], preferred_element_type=F32)
            gy = yz[:, :128].reshape(4, 4, 16, 128)
            gz = yz[:, 128:].reshape(4, 4, 16, 128)
            gx = [
                jnp.stack(x_derivative([field[f][a] for a in range(4)], table, 0)) for f in range(4)
            ]
            scaled = [state[n, :, rows, :] for n in range(6)]
            stiff = state[6, :, rows, :]
            vd = field[3]
            coupled = keep[2, 0, rows, :][None] * vd
            shear = [gy[0] + gx[1], gz[0] + gx[2], gz[1] + gy[2]]
            normal = [gx[0], gy[1], gz[2]]
            trace_sum = 1.5 * (normal[0] + normal[1] + normal[2])
            tensor = [stiff * (trace_sum + 2.0 * normal[n]) + scaled[n] * coupled for n in range(3)]
            tensor += [stiff * shear[n] + scaled[n + 3] * coupled for n in range(3)]
            nodal = state[7, :, rows, :] * vd
            for n in range(3):
                nodal = nodal + scaled[n] * normal[n] + scaled[n + 3] * shear[n]
            flux = gc_length * w_rows()
            along_x = [tensor[0], tensor[3], tensor[4], flux * gx[3]]
            along_y = [tensor[3], tensor[1], tensor[5], flux * gy[3]]
            along_z = [tensor[4], tensor[5], tensor[2], flux * gz[3]]
            y_high, y_low = split(jnp.stack(along_y).reshape(256, 128))
            z_high, z_low = split(jnp.stack(along_z).reshape(256, 128))
            one = jnp.dot(
                jnp.concatenate([y_high, z_high], axis=1), back[...], preferred_element_type=F32
            )
            two = jnp.dot(
                jnp.concatenate([y_low, z_low], axis=1), back[:, :128], preferred_element_type=F32
            )
            total = (one[:, :128] + one[:, 128:] + two).reshape(4, 4, 16, 128)
            for f in range(4):
                tx = jnp.stack(x_derivative([along_x[f][a] for a in range(4)], table, 16))
                result = total[f] + tx
                if f == 3:
                    result = result + nodal
                where = slice(f * 64 + 16 * e, f * 64 + 16 * e + 16)
                summed[:, where, :] = load[:, where, :] - result

    copies[1].wait()
    to_rows(adjoint_b, summed)
    sum_local()
    pack(0)
    pl.semaphore_wait(barrier, len(DIRS))
    messages = send(0)

    copies[2].wait()
    for f in range(3):
        rows = placed(displace_b[f])
        for a in range(4):
            value[a, f * 64 : f * 64 + 64, :] = rows[:, a * 128 : a * 128 + 128]
    for n, (copy, ref) in enumerate(((copies[3], damage_b), (copies[4], history_b))):
        copy.wait()
        rows = placed(ref[...])
        for a in range(4):
            keep[n, a] = rows[:, a * 128 : a * 128 + 128]
    copies[5].wait()
    frozen = jnp.sum(chosen * frozen_b[...].astype(F32), axis=1, keepdims=True)
    keep[2, 0] = jnp.broadcast_to(1.0 - frozen, (64, 128))
    copies[6].wait()
    copies[7].wait()
    state_terms()
    copies[8].wait()
    to_rows(load_b, load)
    copies[9].wait()

    receive(0, messages)

    def half_where(condition, scalar):
        return 1.0 - 0.5 * fmask(condition) * scalar

    inv_z = [
        half_where(lane_k == 7, 1.0) * half_where((lane_k == 0) & (sub > 0), 1.0)
        * half_where((lane_k == 0) & (sub == 0), present[2][-1]),
        half_where(lane_k == 0, 1.0) * half_where((lane_k == 7) & (sub < 7), 1.0)
        * half_where((lane_k == 7) & (sub == 7), present[2][1]),
    ]
    inv_y = []
    for e in range(4):
        lower = 1.0 if e > 0 else present[1][-1]
        upper = 1.0 if e < 3 else present[1][1]
        inv_y.append(half_where(lane_j == 0, lower) * half_where(lane_j == 7, upper))
    inv_x = [half_where(lane_h == 0, present[0][-1]), None, None, half_where(lane_h == 1, present[0][1])]
    for e in range(4):
        for a in range(4):
            scale = jnp.stack([inv_y[e] * inv_z[0], inv_y[e] * inv_z[1]])
            if inv_x[a] is not None:
                scale = scale * inv_x[a]
            scale = scale.reshape(16, 128)
            for f in range(4):
                rows = slice(f * 64 + 16 * e, f * 64 + 16 * e + 16)
                value[a, rows, :] = summed[a, rows, :] * scale

    apply_transposed()
    sum_local()
    pack(1)
    finish(messages)
    messages = send(1)
    receive(1, messages)
    value[...] = value[...] + relaxation * summed[...]

    apply_transposed()
    sum_local()
    pack(2)
    finish(messages)
    messages = send(2)
    receive(2, messages)
    twice = jnp.concatenate([unpick, unpick], axis=1)
    for f in range(4):
        for a in range(4):
            high, low = split(summed[a, f * 64 : f * 64 + 64, :])
            both = jnp.concatenate([high, low], axis=0)
            out_ref[f, :, a * 128 : a * 128 + 128] = jnp.dot(twice, both, preferred_element_type=F32)
    finish(messages)


def shards(adjoint, load, displace, damage, history, frozen, order):
    forward, back, table = (jnp.asarray(c) for c in constants())
    any_spec = pl.BlockSpec(memory_space=pl.ANY)
    return pl.pallas_call(
        kernel,
        out_shape=jax.ShapeDtypeStruct((4, 64, 512), F32),
        in_specs=[any_spec] * 10,
        out_specs=pl.BlockSpec(memory_space=pltpu.VMEM),
        scratch_shapes=[
            pltpu.VMEM((4, 64, 512), BF16),
            pltpu.VMEM((4, 64, 512), BF16),
            pltpu.VMEM((3, 64, 512), BF16),
            pltpu.VMEM((64, 512), BF16),
            pltpu.VMEM((64, 512), BF16),
            pltpu.VMEM((1, 64), jnp.int32),
            pltpu.VMEM((1, 64), jnp.int32),
            pltpu.VMEM((384, 256), BF16),
            pltpu.VMEM((256, 256), BF16),
            pltpu.VMEM((40, 128), F32),
            pltpu.VMEM((4, 256, 128), F32),
            pltpu.VMEM((4, 256, 128), F32),
            pltpu.VMEM((4, 256, 128), F32),
            pltpu.VMEM((8, 4, 64, 128), F32),
            pltpu.VMEM((3, 4, 64, 128), F32),
            pltpu.VMEM((3, 2, 2, 64, 128), F32),
            pltpu.VMEM((3, 2, 2, 16, 128), F32),
            pltpu.VMEM((3, 2, 8, 128), F32),
            pltpu.VMEM((3, 2, 2, 64, 128), F32),
            pltpu.VMEM((3, 2, 2, 16, 128), F32),
            pltpu.VMEM((3, 4, 16, 128), F32),
            pltpu.VMEM((3, 18, 8, 128), F32),
            pltpu.SemaphoreType.DMA((10,)),
            pltpu.SemaphoreType.DMA((3, 26)),
            pltpu.SemaphoreType.DMA((3, 26)),
        ],
        compiler_params=pltpu.CompilerParams(
            collective_id=0, has_side_effects=True, vmem_limit_bytes=32 * 1024 * 1024
        ),
    )(adjoint, load, displace, damage, history, frozen.reshape(1, 64), order, forward, back, table)


def solution(mesh):
    in_specs = (
        P(None, ("gx", "gy", "gz"), None),
        P(None, ("gx", "gy", "gz"), None),
        P(None, ("gx", "gy", "gz"), None),
        P(("gx", "gy", "gz"), None),
        P(("gx", "gy", "gz"), None),
        P(("gx", "gy", "gz")),
        P(("gx", "gy", "gz"), None),
    )
    out_specs = P(None, ("gx", "gy", "gz"), None)
    return jax.shard_map(shards, mesh=mesh, in_specs=in_specs, out_specs=out_specs, check_vma=False)
```

profile of v0, /device:TPU:1, one launch (start us, length us, event | category | flops | bytes accessed | tf_op | source)
XLA Modules:
  0.0 48.1 jit_solution(15770752400686297907)
XLA Ops:
  0.0 0.0 copy-start.9
  0.0 0.0 copy-start.8
  0.0 0.7 %copy-done.9 = s32[1,64]{1,0:T(1,128)S(1)} copy-done((s32[1,64]{1,0:T(1,128)S(1)}, s32[1,64]{1,0:T(1,128)}, u32[]{:S(2)}) %copy-start.9) | copy-done | bytes 280
  0.7 0.0 copy-done.8
  0.7 0.0 copy-start
  0.7 0.9 %copy-done = bf16[4,64,512]{2,1,0:T(8,128)(2,1)S(1)} copy-done((bf16[4,64,512]{2,1,0:T(8,128)(2,1)S(1)}, bf16[4,64,512]{2,1,0:T(8,128)(2,1)}, u32[]{:S(2)}) %copy-start) | copy-done | bytes 262168
  1.6 0.0 copy-start.1
  1.6 0.9 %copy-done.1 = bf16[4,64,512]{2,1,0:T(8,128)(2,1)S(1)} copy-done((bf16[4,64,512]{2,1,0:T(8,128)(2,1)S(1)}, bf16[4,64,512]{2,1,0:T(8,128)(2,1)}, u32[]{:S(2)}) %copy-start.1) | copy-done | bytes 262168
  2.6 0.0 copy-start.2
  2.6 0.9 %copy-done.2 = bf16[3,64,512]{2,1,0:T(8,128)(2,1)S(1)} copy-done((bf16[3,64,512]{2,1,0:T(8,128)(2,1)S(1)}, bf16[3,64,512]{2,1,0:T(8,128)(2,1)}, u32[]{:S(2)}) %copy-start.2) | copy-done | bytes 196632
  3.5 0.0 copy-start.3
  3.5 0.9 %copy-done.3 = bf16[384,256]{1,0:T(8,128)(2,1)S(1)} copy-done((bf16[384,256]{1,0:T(8,128)(2,1)S(1)}, bf16[384,256]{1,0:T(8,128)(2,1)}, u32[]{:S(2)}) %copy-start.3) | copy-done | bytes 196632
  4.4 0.0 copy-start.4
  4.4 0.9 %copy-done.4 = bf16[256,256]{1,0:T(8,128)(2,1)S(1)} copy-done((bf16[256,256]{1,0:T(8,128)(2,1)S(1)}, bf16[256,256]{1,0:T(8,128)(2,1)}, u32[]{:S(2)}) %copy-start.4) | copy-done | bytes 131096
  5.3 0.0 copy-start.5
  5.3 0.8 %copy-done.5 = bf16[64,512]{1,0:T(8,128)(2,1)S(1)} copy-done((bf16[64,512]{1,0:T(8,128)(2,1)S(1)}, bf16[64,512]{1,0:T(8,128)(2,1)}, u32[]{:S(2)}) %copy-start.5) | copy-done | bytes 65560
  6.2 0.0 copy-start.6
  6.2 0.8 %copy-done.6 = bf16[64,512]{1,0:T(8,128)(2,1)S(1)} copy-done((bf16[64,512]{1,0:T(8,128)(2,1)S(1)}, bf16[64,512]{1,0:T(8,128)(2,1)}, u32[]{:S(2)}) %copy-start.6) | copy-done | bytes 65560
  7.0 0.0 copy-start.7
  7.0 0.7 %copy-done.7 = f32[40,128]{1,0:T(8,128)S(1)} copy-done((f32[40,128]{1,0:T(8,128)S(1)}, f32[40,128]{1,0:T(8,128)}, u32[]{:S(2)}) %copy-start.7) | copy-done | bytes 20504
  7.7 39.5 %shard_map.100 = f32[4,64,512]{2,1,0:T(8,128)S(1)} custom-call(bf16[4,64,512]{2,1,0:T(8,128)(2,1)S(1)} %copy-done, bf16[4,64,512]{2,1,0:T(8,128)(2,1)S(1)} %copy-done.1, bf16[3,64,512]{2,1,0:T(8,128)(2,1)S(1)} %copy-done.2, bf16[64,512]{1,0:T(8,128)(2,1)S(1)} %copy-done.5, bf16[64,512]{1,0:T(8,128)(2,1)S(1)} %copy-done.6, s32[1,64]{1,0:T(1,128)S(1)} %bitcast.1, ...), custom_call_target="tpu_custom_call" | custom-call | tf_op jit(solution)/shard_map/pallas_call | solution.py:570
  47.3 0.8 %copy.12 = f32[4,64,512]{2,1,0:T(8,128)} copy(f32[4,64,512]{2,1,0:T(8,128)S(1)} %shard_map.100) | data formatting | bytes 1048576
Async XLA Ops:
  0.0 0.7 %copy-start.9 = (s32[1,64]{1,0:T(1,128)S(1)}, s32[1,64]{1,0:T(1,128)}, u32[]{:S(2)}) copy-start(s32[1,64]{1,0:T(1,128)} %order_h.1) | copy-start | bytes 772
  0.0 0.7 %copy-start.8 = (s32[64]{0:T(128)S(1)}, s32[64]{0:T(128)}, u32[]{:S(2)}) copy-start(s32[64]{0:T(128)} %param.15) | copy-start | bytes 772
  0.7 0.9 %copy-start = (bf16[4,64,512]{2,1,0:T(8,128)(2,1)S(1)}, bf16[4,64,512]{2,1,0:T(8,128)(2,1)}, u32[]{:S(2)}) copy-start(bf16[4,64,512]{2,1,0:T(8,128)(2,1)} %adjoint_h.1) | copy-start | bytes 786436
  1.6 0.9 %copy-start.1 = (bf16[4,64,512]{2,1,0:T(8,128)(2,1)S(1)}, bf16[4,64,512]{2,1,0:T(8,128)(2,1)}, u32[]{:S(2)}) copy-start(bf16[4,64,512]{2,1,0:T(8,128)(2,1)} %load_h.1) | copy-start | bytes 786436
  2.6 0.9 %copy-start.2 = (bf16[3,64,512]{2,1,0:T(8,128)(2,1)S(1)}, bf16[3,64,512]{2,1,0:T(8,128)(2,1)}, u32[]{:S(2)}) copy-start(bf16[3,64,512]{2,1,0:T(8,128)(2,1)} %displace_h.1) | copy-start | bytes 589828
  3.5 0.9 %copy-start.3 = (bf16[384,256]{1,0:T(8,128)(2,1)S(1)}, bf16[384,256]{1,0:T(8,128)(2,1)}, u32[]{:S(2)}) copy-start(bf16[384,256]{1,0:T(8,128)(2,1)} %constant.6.clone.forward_h) | copy-start | bytes 589828
  4.4 0.9 %copy-start.4 = (bf16[256,256]{1,0:T(8,128)(2,1)S(1)}, bf16[256,256]{1,0:T(8,128)(2,1)}, u32[]{:S(2)}) copy-start(bf16[256,256]{1,0:T(8,128)(2,1)} %constant.7.clone.back_h) | copy-start | bytes 393220
  5.3 0.8 %copy-start.5 = (bf16[64,512]{1,0:T(8,128)(2,1)S(1)}, bf16[64,512]{1,0:T(8,128)(2,1)}, u32[]{:S(2)}) copy-start(bf16[64,512]{1,0:T(8,128)(2,1)} %damage_h.1) | copy-start | bytes 196612
  6.2 0.8 %copy-start.6 = (bf16[64,512]{1,0:T(8,128)(2,1)S(1)}, bf16[64,512]{1,0:T(8,128)(2,1)}, u32[]{:S(2)}) copy-start(bf16[64,512]{1,0:T(8,128)(2,1)} %history_h.1) | copy-start | bytes 196612
  7.0 0.7 %copy-start.7 = (f32[40,128]{1,0:T(8,128)S(1)}, f32[40,128]{1,0:T(8,128)}, u32[]{:S(2)}) copy-start(f32[40,128]{1,0:T(8,128)} %constant.8.clone.table_h) | copy-start | bytes 61444
where the time goes:
time: 48.4 us; the launch traced here: 48.1 us
  Pallas kernels  39.5 us (82%)
  local copies, waits for them, and re-layouts  8.53 us (18%)
    pallas_call x1, Pallas kernels, shards(): pl.pallas_call(kernel, out_shape=jax.ShapeDtypeStruct((4, 64, 512), F32),...  39.5 us
    unnamed x21, local copies, waits for them, and re-layouts  8.53 us

commit v1 on v0

v1 whole, which is shorter than its diff:
```python
import jax
import jax.numpy as jnp
import ml_dtypes
import numpy as np
from jax import lax
from jax.experimental import pallas as pl
from jax.experimental.pallas import tpu as pltpu
from jax.sharding import PartitionSpec as P

F32 = jnp.float32
BF16 = jnp.bfloat16
MESH = pl.DeviceIdType.MESH

lame_lambda = 0.15
lame_mu = 0.1
gc_length = 0.3
gc_inverse = 40.0
residual_stiff = 0.001
relaxation = 0.5
gll_points = (
    -1.0,
    -0.8717401485096066,
    -0.5917001814331423,
    -0.2092992179024789,
    0.2092992179024789,
    0.5917001814331423,
    0.8717401485096066,
    1.0,
)

DIRS = [
    (dx, dy, dz)
    for dx in (-1, 0, 1)
    for dy in (-1, 0, 1)
    for dz in (-1, 0, 1)
    if (dx, dy, dz) != (0, 0, 0)
]
X_DIRS = [d for d in DIRS if d[1] == 0 and d[2] == 0]
Y_DIRS = [d for d in DIRS if d[0] == 0 and d[1] != 0 and d[2] == 0]
XY_DIRS = [d for d in DIRS if d[0] != 0 and d[1] != 0 and d[2] == 0]
Z_DIRS = [d for d in DIRS if d[2] != 0]
Z_LATE = [d for d in Z_DIRS if d[1] != 0]
Z_EARLY = [d for d in Z_DIRS if d[1] == 0]
Z_ORDER = sorted(Z_DIRS, key=lambda d: -abs(d[0]) - abs(d[1]))


def legendre_at(points, degree):
    values = []
    for point in points:
        previous = 1.0
        current = point
        for level in range(1, degree):
            following = ((2 * level + 1) * point * current - level * previous) / (level + 1)
            previous = current
            current = following
        values.append(current)
    return values


def gll_tables():
    degree = 7
    points = list(gll_points)
    legendre_vals = legendre_at(points, degree)
    weights = [2.0 / (degree * (degree + 1) * entry * entry) for entry in legendre_vals]
    derivative = []
    for row_index in range(degree + 1):
        row_vals = []
        for col_index in range(degree + 1):
            if row_index != col_index:
                row_vals.append(
                    legendre_vals[row_index]
                    / (legendre_vals[col_index] * (points[row_index] - points[col_index]))
                )
            else:
                row_vals.append(0.0)
        derivative.append(row_vals)
    derivative[0][0] = -degree * (degree + 1) / 4.0
    derivative[degree][degree] = degree * (degree + 1) / 4.0
    return (np.array(weights), np.array(derivative))


def split_np(matrix):
    high = matrix.astype(np.float32).astype(ml_dtypes.bfloat16)
    low = (matrix - high.astype(np.float64)).astype(np.float32).astype(ml_dtypes.bfloat16)
    return high, low


def constants():
    _, derivative = gll_tables()
    eye = np.eye
    forward_y = np.kron(eye(2), np.kron(derivative.T, eye(8)))
    forward_z = np.kron(eye(16), derivative.T)
    back_y = np.kron(eye(2), np.kron(derivative, eye(8)))
    back_z = np.kron(eye(16), derivative)
    f_high, f_low = split_np(np.concatenate([forward_y, forward_z], axis=1))
    forward = np.concatenate([f_high, f_high, f_low], axis=0)
    b_high, b_low = split_np(np.concatenate([back_y, back_z], axis=0))
    back = np.concatenate([b_high, b_low], axis=1)
    swap = np.zeros((2, 2, 64, 2, 2, 64))
    for h in range(2):
        for odd in range(2):
            swap[h, odd, :, odd, h, :] = eye(64)
    swap = swap.reshape(256, 256).astype(ml_dtypes.bfloat16)
    return forward, back, swap


def lane_roll(value, shift):
    shift = shift % 128
    if shift == 0:
        return value
    flat = value.reshape(-1, 128)
    return pltpu.roll(flat, shift, 1).reshape(value.shape)


def lane_swap(value, mask):
    flat = value.reshape(-1, 128)
    index = jnp.bitwise_xor(lax.broadcasted_iota(jnp.int32, flat.shape, 1), mask)
    return jnp.take_along_axis(flat, index, axis=1).reshape(value.shape)


def split(value):
    high = value.astype(BF16)
    low = (value - high.astype(F32)).astype(BF16)
    return high, low


def x_derivative(tiles, matrix):
    even_part = (matrix + matrix[:, ::-1]) / 2
    odd_part = (matrix - matrix[:, ::-1]) / 2
    even = [tiles[n] + tiles[7 - n] for n in range(4)]
    odd = [tiles[n] - tiles[7 - n] for n in range(4)]
    out = [None] * 8
    for n in range(4):
        first = float(even_part[n, 0]) * even[0]
        second = float(odd_part[n, 0]) * odd[0]
        for m in range(1, 4):
            first = first + float(even_part[n, m]) * even[m]
            second = second + float(odd_part[n, m]) * odd[m]
        out[n] = second + first
        out[7 - n] = second - first
    return out


def kernel(
    adjoint_h,
    load_h,
    displace_h,
    damage_h,
    history_h,
    frozen_h,
    order_h,
    forward_h,
    back_h,
    swap_h,
    out_ref,
    adjoint_b,
    load_b,
    displace_b,
    damage_b,
    history_b,
    frozen_b,
    order_b,
    forward,
    back,
    swap,
    value,
    kept,
    load,
    summed,
    state,
    keep,
    ys,
    zs,
    xr,
    yr,
    xyr,
    zr,
    in_sem,
    send_sem,
    recv_sem,
):
    weights, derivative = gll_tables()
    px, py, pz = (lax.axis_index("gx"), lax.axis_index("gy"), lax.axis_index("gz"))
    sizes = (lax.axis_size("gx"), lax.axis_size("gy"), lax.axis_size("gz"))

    pairs = (
        (order_h, order_b),
        (adjoint_h, adjoint_b),
        (swap_h, swap),
        (displace_h, displace_b),
        (forward_h, forward),
        (damage_h, damage_b),
        (history_h, history_b),
        (frozen_h, frozen_b),
        (load_h, load_b),
        (back_h, back),
    )
    copies = [pltpu.make_async_copy(src, dst, in_sem.at[n]) for n, (src, dst) in enumerate(pairs)]
    for copy in copies[:3]:
        copy.start()

    along = [
        {
            -1: lax.rem(p + n - 1, n),
            0: p,
            1: lax.rem(p + 1, n),
        }
        for p, n in zip((px, py, pz), sizes)
    ]

    def target(d):
        return tuple(along[axis][d[axis]] for axis in range(3))

    barrier = pltpu.get_barrier_semaphore()
    for d in DIRS:
        pl.semaphore_signal(barrier, inc=1, device_id=target(d), device_id_type=MESH)
    for copy in copies[3:]:
        copy.start()

    present = [
        {
            -1: (p > 0).astype(F32),
            1: (p < n - 1).astype(F32),
        }
        for p, n in zip((px, py, pz), sizes)
    ]

    lane = lax.broadcasted_iota(jnp.int32, (8, 128), 1)
    sub = lax.broadcasted_iota(jnp.int32, (8, 128), 0)
    lane_k = lane % 8
    lane_j = (lane // 8) % 8
    lane_h = lane // 64

    def fmask(condition):
        return jnp.where(condition, 1.0, 0.0).astype(F32)

    j_end = {-1: fmask(lane_j == 0), 1: fmask(lane_j == 7)}
    h_end = {-1: fmask(lane_h == 0), 1: fmask(lane_h == 1)}
    first_z = (lane_h == 0) & (lane_k == 0)
    last_z = (lane_h == 1) & (lane_k == 7)
    z_end = {-1: fmask(first_z), 1: fmask(last_z)}
    inner_z = ((lane_h == 0) & (lane_k == 7)) | ((lane_h == 1) & (lane_k == 0))
    z_here = fmask(inner_z | (last_z & (sub < 7)))
    z_next = fmask(first_z & (sub > 0))

    copies[0].wait()
    row_id = lax.broadcasted_iota(jnp.int32, (64, 64), 0)
    place = ((row_id // 8) % 4) * 16 + 2 * (row_id % 8) + row_id // 32
    chosen = fmask(place == order_b[...])
    pick = chosen.astype(BF16)
    unpick = chosen.T.astype(BF16)

    def to_tiles(stored):
        rows = jnp.dot(pick, stored, preferred_element_type=F32).astype(BF16)
        sides = jnp.stack(
            [
                jnp.concatenate([rows[:32, n : n + 128], rows[32:, n : n + 128]], axis=1)
                for n in range(0, 512, 128)
            ]
        )
        tiles = jnp.dot(sides.reshape(128, 256), swap[...], preferred_element_type=F32)
        return tiles.reshape(4, 32, 256)

    def put_tiles(tiles, ref, start):
        for a in range(4):
            ref[2 * a, start : start + 32, :] = tiles[a, :, :128]
            ref[2 * a + 1, start : start + 32, :] = tiles[a, :, 128:]

    def group(ref, e):
        return jnp.stack([ref[:, f * 32 + 8 * e : f * 32 + 8 * e + 8, :] for f in range(4)], axis=1)

    def put_group(ref, e, block):
        for f in range(4):
            ref[:, f * 32 + 8 * e : f * 32 + 8 * e + 8, :] = block[:, f]

    def sum_z(block):
        flat = block.reshape(-1, 8, 128)
        taken = lane_swap(jnp.where(first_z, pltpu.roll(flat, 7, 1), flat), 71)
        total = flat + z_here * taken + z_next * pltpu.roll(taken, 1, 1)
        return total.reshape(block.shape)

    def sum_y(e):
        here, beyond = group(summed, e), group(summed, e + 1)
        taken = lane_swap(jnp.where(lane_j == 7, here, beyond), 56)
        put_group(summed, e, here + j_end[1] * taken)
        put_group(summed, e + 1, beyond + j_end[-1] * taken)

    def pack_z(r):
        for n, (row, h, k) in enumerate(((0, 0, 0), (7, 1, 7))):
            packed = jnp.zeros((8, 128), F32)
            for slot in range(16):
                i, half = slot // 2, slot % 2
                piece = summed[i, pl.ds(half * 64 + row, 8, stride=8), :]
                moved = lane_roll(piece, (slot // 8 - h) * 64 + slot % 8 - k)
                packed = jnp.where((lane_h == slot // 8) & (lane_k == slot % 8), moved, packed)
            zs[r, n] = packed

    def pack_y(r):
        for n, (e, j) in enumerate(((0, 0), (3, 7))):
            for g in range(4):
                packed = jnp.zeros((8, 128), F32)
                for slot in range(8):
                    row = (slot // 2) * 32 + 8 * e
                    piece = summed[2 * g + slot % 2, row : row + 8, :]
                    packed = jnp.where(lane_j == slot, lane_roll(piece, 8 * (slot - j)), packed)
                ys[r, n, g] = packed

    def message(r, d):
        n = DIRS.index(d)
        dx, dy, dz = d
        if d in X_DIRS:
            src, dst = summed.at[7 if dx > 0 else 0], xr.at[r, (dx + 1) // 2]
        elif d in Y_DIRS:
            src, dst = ys.at[r, (dy + 1) // 2], yr.at[r, (dy + 1) // 2]
        elif d in XY_DIRS:
            src, dst = ys.at[r, (dy + 1) // 2, 3 if dx > 0 else 0], xyr.at[r, XY_DIRS.index(d)]
        else:
            src, dst = zs.at[r, (dz + 1) // 2], zr.at[r, Z_DIRS.index(d)]
        return pltpu.make_async_remote_copy(
            src_ref=src,
            dst_ref=dst,
            send_sem=send_sem.at[r, n],
            recv_sem=recv_sem.at[r, n],
            device_id=target(d),
            device_id_type=MESH,
        )

    def send(r, messages, dirs):
        for d in dirs:
            messages[d] = message(r, d)
            messages[d].start()

    def finish(messages):
        for d in DIRS:
            messages[d].wait_send()

    def add_z(r, messages, dirs):
        for dz in (-1, 1):
            side = -dz
            face = None
            for d in dirs:
                if d[2] != dz:
                    continue
                messages[d].wait_recv()
                part = zr[r, Z_DIRS.index(d)]
                dx, dy, _ = d
                wanted = None
                if dx != 0:
                    slots = (lane_k < 2) if dx > 0 else (lane_k >= 6)
                    wanted = h_end[-dx] * fmask(slots) * present[0][-dx]
                if dy != 0:
                    mine = j_end[-dy] * fmask(sub % 4 == (0 if dy > 0 else 3)) * present[1][-dy]
                    wanted = mine if wanted is None else wanted * mine
                    part = pltpu.roll(part, (-3 * dy) % 8, 0)
                part = lane_roll(part, -70 * dx - 56 * dy)
                if wanted is not None:
                    part = part * wanted
                face = part if face is None else face + part
            row, h, k = (0, 0, 0) if side < 0 else (7, 1, 7)
            wanted = z_end[side] * present[2][side]
            for slot in range(16):
                i, half = slot // 2, slot % 2
                where = pl.ds(half * 64 + row, 8, stride=8)
                moved = lane_roll(face, (h - slot // 8) * 64 + k - slot % 8)
                value[i, where, :] = value[i, where, :] + moved * wanted

    def receive_early(r, messages):
        for i in range(1, 7):
            value[i] = summed[i]
        for d in X_DIRS:
            messages[d].wait_recv()
            i = 0 if d[0] > 0 else 7
            value[i] = summed[i] + xr[r, (d[0] + 1) // 2] * present[0][-d[0]]
        add_z(r, messages, Z_EARLY)

    def receive_late(r, messages):
        for d in Y_DIRS:
            messages[d].wait_recv()
            dy = d[1]
            side = -dy
            faces = [yr[r, (dy + 1) // 2, g] for g in range(4)]
            for dx in (-1, 1):
                e = (dx, dy, 0)
                messages[e].wait_recv()
                edge = lane_roll(xyr[r, XY_DIRS.index(e)], -8 * dx)
                wanted = fmask(lane_j % 2 == (0 if dx > 0 else 1)) * present[0][-dx]
                g = 0 if dx > 0 else 3
                faces[g] = faces[g] + edge * wanted
            e, j = (0, 0) if side < 0 else (3, 7)
            wanted = j_end[side] * present[1][side]
            for i in range(8):
                for f in range(4):
                    slot = f * 2 + i % 2
                    row = f * 32 + 8 * e
                    moved = lane_roll(faces[i // 2], 8 * (j - slot))
                    value[i, row : row + 8, :] = value[i, row : row + 8, :] + moved * wanted
        add_z(r, messages, Z_LATE)

    def brick():
        line_j = jnp.zeros((8, 128), F32)
        line_k = jnp.zeros((8, 128), F32)
        for n in range(8):
            line_j = jnp.where(lane_j == n, float(weights[n]), line_j)
            line_k = jnp.where(lane_k == n, float(weights[n]), line_k)
        plane = line_j * line_k
        return jnp.stack([plane * float(weights[n]) for n in range(8)])

    def gradients(block, count, exact):
        if exact:
            high = block.reshape(count * 64, 128).astype(BF16)
            left, table = jnp.concatenate([high, high], axis=1), forward[128:384, :]
        else:
            high, low = split(block.reshape(count * 64, 128))
            left, table = jnp.concatenate([high, low, high], axis=1), forward[...]
        yz = jnp.dot(left, table, preferred_element_type=F32)
        gx = jnp.stack(x_derivative([block[i] for i in range(8)], derivative))
        return gx, yz[:, :128].reshape(block.shape), yz[:, 128:].reshape(block.shape)

    def state_terms(e):
        rows = slice(8 * e, 8 * e + 8)
        moved = jnp.stack(
            [value[:, f * 32 + 8 * e : f * 32 + 8 * e + 8, :] for f in range(3)], axis=1
        )
        gx, gy, gz = gradients(moved, 3, True)
        shear = [gy[:, 0] + gx[:, 1], gz[:, 0] + gx[:, 2], gz[:, 1] + gy[:, 2]]
        normal = [gx[:, 0], gy[:, 1], gz[:, 2]]
        trace_sum = normal[0] + normal[1] + normal[2]
        stress = [lame_lambda * trace_sum + 2.0 * lame_mu * n for n in normal]
        stress += [lame_mu * s for s in shear]
        energy = stress[0] * normal[0] + stress[1] * normal[1] + stress[2] * normal[2]
        energy = 0.5 * (energy + stress[3] * shear[0] + stress[4] * shear[1] + stress[5] * shear[2])
        loading = keep[2, 0, rows, :][None]
        driving = (1.0 - loading) * keep[1, :, rows, :] + loading * energy
        intact = 1.0 - keep[0, :, rows, :]
        mass = brick()
        slope = -2.0 * intact * mass
        for n in range(6):
            state[n, :, rows, :] = slope * stress[n]
        state[6, :, rows, :] = lame_mu * mass * (intact * intact + residual_stiff)
        state[7, :, rows, :] = mass * (gc_inverse + 2.0 * driving)

    def apply_transposed(e, block):
        rows = slice(8 * e, 8 * e + 8)
        gx, gy, gz = gradients(block, 4, False)
        scaled = [state[n, :, rows, :] for n in range(6)]
        stiff = state[6, :, rows, :]
        vd = block[:, 3]
        coupled = keep[2, 0, rows, :][None] * vd
        shear = [gy[:, 0] + gx[:, 1], gz[:, 0] + gx[:, 2], gz[:, 1] + gy[:, 2]]
        normal = [gx[:, 0], gy[:, 1], gz[:, 2]]
        trace_sum = 1.5 * (normal[0] + normal[1] + normal[2])
        tensor = [stiff * (trace_sum + 2.0 * normal[n]) + scaled[n] * coupled for n in range(3)]
        tensor += [stiff * shear[n] + scaled[n + 3] * coupled for n in range(3)]
        nodal = state[7, :, rows, :] * vd
        for n in range(3):
            nodal = nodal + scaled[n] * normal[n] + scaled[n + 3] * shear[n]
        flux = gc_length * brick()
        along_x = jnp.stack([tensor[0], tensor[3], tensor[4], flux * gx[:, 3]], axis=1)
        along_y = jnp.stack([tensor[3], tensor[1], tensor[5], flux * gy[:, 3]], axis=1)
        along_z = jnp.stack([tensor[4], tensor[5], tensor[2], flux * gz[:, 3]], axis=1)
        y_high, y_low = split(along_y.reshape(256, 128))
        z_high, z_low = split(along_z.reshape(256, 128))
        one = jnp.dot(
            jnp.concatenate([y_high, z_high], axis=1), back[...], preferred_element_type=F32
        )
        two = jnp.dot(
            jnp.concatenate([y_low, z_low], axis=1), back[:, :128], preferred_element_type=F32
        )
        total = (one[:, :128] + one[:, 128:] + two).reshape(8, 4, 8, 128)
        total = total + jnp.stack(x_derivative([along_x[i] for i in range(8)], derivative.T))
        result = group(load, e) - total
        result = jnp.concatenate([result[:, :3], (result[:, 3] - nodal)[:, None]], axis=1)
        put_group(summed, e, sum_z(result))

    def ship(r):
        messages = {}
        pack_z(r)
        if r == 0:
            pl.semaphore_wait(barrier, len(DIRS))
        send(r, messages, Z_ORDER)
        send(r, messages, X_DIRS)
        pack_y(r)
        send(r, messages, XY_DIRS + Y_DIRS)
        return messages

    copies[1].wait()
    copies[2].wait()
    for f in range(4):
        put_tiles(to_tiles(adjoint_b[f]), summed, f * 32)
    for e in range(4):
        put_group(summed, e, sum_z(group(summed, e)))
    for e in range(3):
        sum_y(e)
    messages = ship(0)

    copies[3].wait()
    for f in range(3):
        put_tiles(to_tiles(displace_b[f]), value, f * 32)
    copies[4].wait()
    copies[5].wait()
    put_tiles(to_tiles(damage_b[...]), keep.at[0], 0)
    copies[6].wait()
    put_tiles(to_tiles(history_b[...]), keep.at[1], 0)
    copies[7].wait()
    frozen = 1.0 - jnp.sum(chosen * frozen_b[...].astype(F32), axis=1, keepdims=True)
    low_half = lax.broadcasted_iota(jnp.int32, (32, 128), 1) < 64
    keep[2, 0] = jnp.where(low_half, frozen[:32], frozen[32:])
    for e in range(4):
        state_terms(e)
    copies[8].wait()
    for f in range(4):
        put_tiles(to_tiles(load_b[f]), load, f * 32)
    copies[9].wait()

    def halved(condition, scalar):
        return 1.0 - 0.5 * fmask(condition) * scalar

    inv_z = halved(inner_z, 1.0) * halved(first_z & (sub > 0), 1.0) * halved(last_z & (sub < 7), 1.0)
    inv_z = inv_z * halved(first_z & (sub == 0), present[2][-1]) * halved(last_z & (sub == 7), present[2][1])

    def average(e):
        lower = 1.0 if e > 0 else present[1][-1]
        upper = 1.0 if e < 3 else present[1][1]
        scale = inv_z * halved(lane_j == 0, lower) * halved(lane_j == 7, upper)
        scales = [scale] * 8
        scales[0] = scale * (1.0 - 0.5 * present[0][-1])
        scales[7] = scale * (1.0 - 0.5 * present[0][1])
        block = group(value, e) * jnp.stack(scales)[:, None]
        put_group(kept, e, block)
        return block

    def relax(e):
        return group(kept, e) + relaxation * group(value, e)

    for r, ready in ((0, average), (1, relax)):
        receive_early(r, messages)
        finish(messages)
        early = [ready(e) for e in (1, 2)]
        for e in (1, 2):
            apply_transposed(e, early[e - 1])
        sum_y(1)
        receive_late(r, messages)
        for e in (0, 3):
            apply_transposed(e, ready(e))
        sum_y(0)
        sum_y(2)
        messages = ship(r + 1)

    receive_early(2, messages)
    receive_late(2, messages)
    twice = jnp.concatenate([unpick, unpick], axis=1)
    for f in range(4):
        rows = slice(f * 32, f * 32 + 32)
        sides = jnp.stack(
            [jnp.concatenate([value[2 * a, rows, :], value[2 * a + 1, rows, :]], axis=1) for a in range(4)]
        )
        high, low = split(sides.reshape(128, 256))
        both = jnp.concatenate([high, low], axis=0)
        moved = jnp.dot(both, swap[...], preferred_element_type=F32).astype(BF16)
        for a in range(4):
            parts = []
            for n in (a * 32, 128 + a * 32):
                parts += [moved[n : n + 32, :128], moved[n : n + 32, 128:]]
            stacked = jnp.concatenate(parts, axis=0)
            out_ref[f, :, a * 128 : a * 128 + 128] = jnp.dot(
                twice, stacked, preferred_element_type=F32
            )
    finish(messages)


def shards(adjoint, load, displace, damage, history, frozen, order):
    forward, back, swap = (jnp.asarray(c) for c in constants())
    hbm = pl.BlockSpec(memory_space=pltpu.HBM)
    return pl.pallas_call(
        kernel,
        out_shape=jax.ShapeDtypeStruct((4, 64, 512), F32),
        in_specs=[hbm] * 10,
        out_specs=pl.BlockSpec(memory_space=pltpu.VMEM),
        scratch_shapes=[
            pltpu.VMEM((4, 64, 512), BF16),
            pltpu.VMEM((4, 64, 512), BF16),
            pltpu.VMEM((3, 64, 512), BF16),
            pltpu.VMEM((64, 512), BF16),
            pltpu.VMEM((64, 512), BF16),
            pltpu.VMEM((1, 64), jnp.int32),
            pltpu.VMEM((1, 64), jnp.int32),
            pltpu.VMEM((384, 256), BF16),
            pltpu.VMEM((256, 256), BF16),
            pltpu.VMEM((256, 256), BF16),
            pltpu.VMEM((8, 128, 128), F32),
            pltpu.VMEM((8, 128, 128), F32),
            pltpu.VMEM((8, 128, 128), F32),
            pltpu.VMEM((8, 128, 128), F32),
            pltpu.VMEM((8, 8, 32, 128), F32),
            pltpu.VMEM((3, 8, 32, 128), F32),
            pltpu.VMEM((3, 2, 4, 8, 128), F32),
            pltpu.VMEM((3, 2, 8, 128), F32),
            pltpu.VMEM((3, 2, 128, 128), F32),
            pltpu.VMEM((3, 2, 4, 8, 128), F32),
            pltpu.VMEM((3, 4, 8, 128), F32),
            pltpu.VMEM((3, 18, 8, 128), F32),
            pltpu.SemaphoreType.DMA((10,)),
            pltpu.SemaphoreType.DMA((3, 26)),
            pltpu.SemaphoreType.DMA((3, 26)),
        ],
        compiler_params=pltpu.CompilerParams(
            collective_id=0, has_side_effects=True, vmem_limit_bytes=32 * 1024 * 1024
        ),
    )(adjoint, load, displace, damage, history, frozen.reshape(1, 64), order, forward, back, swap)


def solution(mesh):
    in_specs = (
        P(None, ("gx", "gy", "gz"), None),
        P(None, ("gx", "gy", "gz"), None),
        P(None, ("gx", "gy", "gz"), None),
        P(("gx", "gy", "gz"), None),
        P(("gx", "gy", "gz"), None),
        P(("gx", "gy", "gz")),
        P(("gx", "gy", "gz"), None),
    )
    out_specs = P(None, ("gx", "gy", "gz"), None)
    return jax.shard_map(shards, mesh=mesh, in_specs=in_specs, out_specs=out_specs, check_vma=False)
```

time: 48.4 us -> 43.6 us (0.901)
  Pallas kernels: 39.5 us -> 34.5 us
    pallas_call x1, Pallas kernels: 39.5 us -> 34.5 us  [shards(): pl.pallas_call(kernel, out_shape=jax.ShapeDtypeStruct((4, 64, 512), F32),...]
where the time goes in v1:
time: 43.6 us; the launch traced here: 43.2 us
  Pallas kernels  34.5 us (79%)
  local copies, waits for them, and re-layouts  8.7 us (20%)
    pallas_call x1, Pallas kernels, shards(): pl.pallas_call(kernel, out_shape=jax.ShapeDtypeStruct((4, 64, 512), F32),...  34.5 us
    unnamed x21, local copies, waits for them, and re-layouts  8.7 us

profile of v1, /device:TPU:1, one launch (start us, length us, event | category | flops | bytes accessed | tf_op | source)
XLA Modules:
  0.0 43.2 jit_solution(14903036544303834062)
XLA Ops:
  0.0 0.0 copy-start.9
  0.0 0.0 copy-start.8
  0.0 0.7 %copy-done.9 = s32[1,64]{1,0:T(1,128)S(1)} copy-done((s32[1,64]{1,0:T(1,128)S(1)}, s32[1,64]{1,0:T(1,128)}, u32[]{:S(2)}) %copy-start.9) | copy-done | bytes 280
  0.7 0.0 copy-done.8
  0.7 0.0 copy-start
  0.7 0.9 %copy-done = bf16[4,64,512]{2,1,0:T(8,128)(2,1)S(1)} copy-done((bf16[4,64,512]{2,1,0:T(8,128)(2,1)S(1)}, bf16[4,64,512]{2,1,0:T(8,128)(2,1)}, u32[]{:S(2)}) %copy-start) | copy-done | bytes 262168
  1.6 0.0 copy-start.1
  1.6 0.9 %copy-done.1 = bf16[4,64,512]{2,1,0:T(8,128)(2,1)S(1)} copy-done((bf16[4,64,512]{2,1,0:T(8,128)(2,1)S(1)}, bf16[4,64,512]{2,1,0:T(8,128)(2,1)}, u32[]{:S(2)}) %copy-start.1) | copy-done | bytes 262168
  2.6 0.0 copy-start.2
  2.6 0.9 %copy-done.2 = bf16[3,64,512]{2,1,0:T(8,128)(2,1)S(1)} copy-done((bf16[3,64,512]{2,1,0:T(8,128)(2,1)S(1)}, bf16[3,64,512]{2,1,0:T(8,128)(2,1)}, u32[]{:S(2)}) %copy-start.2) | copy-done | bytes 196632
  3.5 0.0 copy-start.3
  3.5 0.9 %copy-done.3 = bf16[384,256]{1,0:T(8,128)(2,1)S(1)} copy-done((bf16[384,256]{1,0:T(8,128)(2,1)S(1)}, bf16[384,256]{1,0:T(8,128)(2,1)}, u32[]{:S(2)}) %copy-start.3) | copy-done | bytes 196632
  4.4 0.0 copy-start.4
  4.4 0.9 %copy-done.4 = bf16[256,256]{1,0:T(8,128)(2,1)S(1)} copy-done((bf16[256,256]{1,0:T(8,128)(2,1)S(1)}, bf16[256,256]{1,0:T(8,128)(2,1)}, u32[]{:S(2)}) %copy-start.4) | copy-done | bytes 131096
  5.3 0.0 copy-start.5
  5.3 0.9 %copy-done.5 = bf16[256,256]{1,0:T(8,128)(2,1)S(1)} copy-done((bf16[256,256]{1,0:T(8,128)(2,1)S(1)}, bf16[256,256]{1,0:T(8,128)(2,1)}, u32[]{:S(2)}) %copy-start.5) | copy-done | bytes 131096
  6.2 0.0 copy-start.6
  6.2 0.8 %copy-done.6 = bf16[64,512]{1,0:T(8,128)(2,1)S(1)} copy-done((bf16[64,512]{1,0:T(8,128)(2,1)S(1)}, bf16[64,512]{1,0:T(8,128)(2,1)}, u32[]{:S(2)}) %copy-start.6) | copy-done | bytes 65560
  7.1 0.0 copy-start.7
  7.1 0.8 %copy-done.7 = bf16[64,512]{1,0:T(8,128)(2,1)S(1)} copy-done((bf16[64,512]{1,0:T(8,128)(2,1)S(1)}, bf16[64,512]{1,0:T(8,128)(2,1)}, u32[]{:S(2)}) %copy-start.7) | copy-done | bytes 65560
  7.9 34.5 %shard_map.100 = f32[4,64,512]{2,1,0:T(8,128)S(1)} custom-call(bf16[4,64,512]{2,1,0:T(8,128)(2,1)S(1)} %copy-done, bf16[4,64,512]{2,1,0:T(8,128)(2,1)S(1)} %copy-done.1, bf16[3,64,512]{2,1,0:T(8,128)(2,1)S(1)} %copy-done.2, bf16[64,512]{1,0:T(8,128)(2,1)S(1)} %copy-done.6, bf16[64,512]{1,0:T(8,128)(2,1)S(1)} %copy-done.7, s32[1,64]{1,0:T(1,128)S(1)} %bitcast.1, ...), custom_call_target="tpu_custom_call" | custom-call | tf_op jit(solution)/shard_map/pallas_call | solution.py:574
  42.5 0.8 %copy.12 = f32[4,64,512]{2,1,0:T(8,128)} copy(f32[4,64,512]{2,1,0:T(8,128)S(1)} %shard_map.100) | data formatting | bytes 1048576
Async XLA Ops:
  0.0 0.7 %copy-start.9 = (s32[1,64]{1,0:T(1,128)S(1)}, s32[1,64]{1,0:T(1,128)}, u32[]{:S(2)}) copy-start(s32[1,64]{1,0:T(1,128)} %order_h.1) | copy-start | bytes 772
  0.0 0.7 %copy-start.8 = (s32[64]{0:T(128)S(1)}, s32[64]{0:T(128)}, u32[]{:S(2)}) copy-start(s32[64]{0:T(128)} %param.15) | copy-start | bytes 772
  0.7 0.9 %copy-start = (bf16[4,64,512]{2,1,0:T(8,128)(2,1)S(1)}, bf16[4,64,512]{2,1,0:T(8,128)(2,1)}, u32[]{:S(2)}) copy-start(bf16[4,64,512]{2,1,0:T(8,128)(2,1)} %adjoint_h.1) | copy-start | bytes 786436
  1.6 0.9 %copy-start.1 = (bf16[4,64,512]{2,1,0:T(8,128)(2,1)S(1)}, bf16[4,64,512]{2,1,0:T(8,128)(2,1)}, u32[]{:S(2)}) copy-start(bf16[4,64,512]{2,1,0:T(8,128)(2,1)} %load_h.1) | copy-start | bytes 786436
  2.6 0.9 %copy-start.2 = (bf16[3,64,512]{2,1,0:T(8,128)(2,1)S(1)}, bf16[3,64,512]{2,1,0:T(8,128)(2,1)}, u32[]{:S(2)}) copy-start(bf16[3,64,512]{2,1,0:T(8,128)(2,1)} %displace_h.1) | copy-start | bytes 589828
  3.5 0.9 %copy-start.3 = (bf16[384,256]{1,0:T(8,128)(2,1)S(1)}, bf16[384,256]{1,0:T(8,128)(2,1)}, u32[]{:S(2)}) copy-start(bf16[384,256]{1,0:T(8,128)(2,1)} %constant.6.clone.forward_h) | copy-start | bytes 589828
  4.4 0.9 %copy-start.4 = (bf16[256,256]{1,0:T(8,128)(2,1)S(1)}, bf16[256,256]{1,0:T(8,128)(2,1)}, u32[]{:S(2)}) copy-start(bf16[256,256]{1,0:T(8,128)(2,1)} %constant.8.clone.swap_h) | copy-start | bytes 393220
  5.3 0.9 %copy-start.5 = (bf16[256,256]{1,0:T(8,128)(2,1)S(1)}, bf16[256,256]{1,0:T(8,128)(2,1)}, u32[]{:S(2)}) copy-start(bf16[256,256]{1,0:T(8,128)(2,1)} %constant.7.clone.back_h) | copy-start | bytes 393220
  6.2 0.8 %copy-start.6 = (bf16[64,512]{1,0:T(8,128)(2,1)S(1)}, bf16[64,512]{1,0:T(8,128)(2,1)}, u32[]{:S(2)}) copy-start(bf16[64,512]{1,0:T(8,128)(2,1)} %damage_h.1) | copy-start | bytes 196612
  7.1 0.8 %copy-start.7 = (bf16[64,512]{1,0:T(8,128)(2,1)S(1)}, bf16[64,512]{1,0:T(8,128)(2,1)}, u32[]{:S(2)}) copy-start(bf16[64,512]{1,0:T(8,128)(2,1)} %history_h.1) | copy-start | bytes 196612

commit v2 on v1

--- a/solution.py
+++ b/solution.py
@@ -27,6 +27,9 @@
     0.8717401485096066,
     1.0,
 )
+
+EY = (0, 3, 1, 2)
+TILE = (0, 2, 3, 1)
 
 DIRS = [
     (dx, dy, dz)
@@ -245,33 +248,38 @@
 
     copies[0].wait()
     row_id = lax.broadcasted_iota(jnp.int32, (64, 64), 0)
-    place = ((row_id // 8) % 4) * 16 + 2 * (row_id % 8) + row_id // 32
+    tile_id = (row_id // 8) % 4
+    row_ey = jnp.where(tile_id == 1, 3, jnp.where(tile_id > 1, tile_id - 1, 0))
+    place = row_ey * 16 + 2 * (row_id % 8) + row_id // 32
     chosen = fmask(place == order_b[...])
     pick = chosen.astype(BF16)
     unpick = chosen.T.astype(BF16)
 
-    def to_tiles(stored):
-        rows = jnp.dot(pick, stored, preferred_element_type=F32).astype(BF16)
-        sides = jnp.stack(
-            [
-                jnp.concatenate([rows[:32, n : n + 128], rows[32:, n : n + 128]], axis=1)
-                for n in range(0, 512, 128)
-            ]
+    def to_tiles(fields):
+        sides = []
+        for stored in fields:
+            rows = jnp.dot(pick, stored, preferred_element_type=F32).astype(BF16)
+            for n in range(0, 512, 128):
+                sides.append(jnp.concatenate([rows[:32, n : n + 128], rows[32:, n : n + 128]], axis=1))
+        tiles = jnp.dot(
+            jnp.concatenate(sides, axis=0), swap[...], preferred_element_type=F32
         )
-        tiles = jnp.dot(sides.reshape(128, 256), swap[...], preferred_element_type=F32)
-        return tiles.reshape(4, 32, 256)
-
-    def put_tiles(tiles, ref, start):
-        for a in range(4):
-            ref[2 * a, start : start + 32, :] = tiles[a, :, :128]
-            ref[2 * a + 1, start : start + 32, :] = tiles[a, :, 128:]
-
-    def group(ref, e):
-        return jnp.stack([ref[:, f * 32 + 8 * e : f * 32 + 8 * e + 8, :] for f in range(4)], axis=1)
-
-    def put_group(ref, e, block):
+        return tiles.reshape(len(fields) * 4, 32, 256)
+
+    def put_tiles(tiles, places):
+        for n, (ref, start) in enumerate(places):
+            for a in range(4):
+                ref[2 * a, start : start + 32, :] = tiles[4 * n + a, :, :128]
+                ref[2 * a + 1, start : start + 32, :] = tiles[4 * n + a, :, 128:]
+
+    def group(ref, start, rows, fields=4):
+        return jnp.stack(
+            [ref[:, f * 32 + start : f * 32 + start + rows, :] for f in range(fields)], axis=1
+        )
+
+    def put_group(ref, start, rows, block):
         for f in range(4):
-            ref[:, f * 32 + 8 * e : f * 32 + 8 * e + 8, :] = block[:, f]
+            ref[:, f * 32 + start : f * 32 + start + rows, :] = block[:, f]
 
     def sum_z(block):
         flat = block.reshape(-1, 8, 128)
@@ -280,10 +288,11 @@
         return total.reshape(block.shape)
 
     def sum_y(e):
-        here, beyond = group(summed, e), group(summed, e + 1)
+        lower, upper = 8 * TILE[e], 8 * TILE[e + 1]
+        here, beyond = group(summed, lower, 8), group(summed, upper, 8)
         taken = lane_swap(jnp.where(lane_j == 7, here, beyond), 56)
-        put_group(summed, e, here + j_end[1] * taken)
-        put_group(summed, e + 1, beyond + j_end[-1] * taken)
+        put_group(summed, lower, 8, here + j_end[1] * taken)
+        put_group(summed, upper, 8, beyond + j_end[-1] * taken)
 
     def pack_z(r):
         for n, (row, h, k) in enumerate(((0, 0, 0), (7, 1, 7))):
@@ -296,11 +305,11 @@
             zs[r, n] = packed
 
     def pack_y(r):
-        for n, (e, j) in enumerate(((0, 0), (3, 7))):
+        for n, (t, j) in enumerate(((0, 0), (1, 7))):
             for g in range(4):
                 packed = jnp.zeros((8, 128), F32)
                 for slot in range(8):
-                    row = (slot // 2) * 32 + 8 * e
+                    row = (slot // 2) * 32 + 8 * t
                     piece = summed[2 * g + slot % 2, row : row + 8, :]
                     packed = jnp.where(lane_j == slot, lane_roll(piece, 8 * (slot - j)), packed)
                 ys[r, n, g] = packed
@@ -349,9 +358,9 @@
                     slots = (lane_k < 2) if dx > 0 else (lane_k >= 6)
                     wanted = h_end[-dx] * fmask(slots) * present[0][-dx]
                 if dy != 0:
-                    mine = j_end[-dy] * fmask(sub % 4 == (0 if dy > 0 else 3)) * present[1][-dy]
+                    mine = j_end[-dy] * fmask(sub % 4 == (0 if dy > 0 else 1)) * present[1][-dy]
                     wanted = mine if wanted is None else wanted * mine
-                    part = pltpu.roll(part, (-3 * dy) % 8, 0)
+                    part = pltpu.roll(part, -dy % 8, 0)
                 part = lane_roll(part, -70 * dx - 56 * dy)
                 if wanted is not None:
                     part = part * wanted
@@ -386,12 +395,12 @@
                 wanted = fmask(lane_j % 2 == (0 if dx > 0 else 1)) * present[0][-dx]
                 g = 0 if dx > 0 else 3
                 faces[g] = faces[g] + edge * wanted
-            e, j = (0, 0) if side < 0 else (3, 7)
+            t, j = (0, 0) if side < 0 else (1, 7)
             wanted = j_end[side] * present[1][side]
             for i in range(8):
                 for f in range(4):
                     slot = f * 2 + i % 2
-                    row = f * 32 + 8 * e
+                    row = f * 32 + 8 * t
                     moved = lane_roll(faces[i // 2], 8 * (j - slot))
                     value[i, row : row + 8, :] = value[i, row : row + 8, :] + moved * wanted
         add_z(r, messages, Z_LATE)
@@ -402,26 +411,24 @@
         for n in range(8):
             line_j = jnp.where(lane_j == n, float(weights[n]), line_j)
             line_k = jnp.where(lane_k == n, float(weights[n]), line_k)
-        plane = line_j * line_k
+        plane = (line_j * line_k)[:1]
         return jnp.stack([plane * float(weights[n]) for n in range(8)])
 
-    def gradients(block, count, exact):
+    def gradients(block, exact):
         if exact:
-            high = block.reshape(count * 64, 128).astype(BF16)
+            high = block.reshape(-1, 128).astype(BF16)
             left, table = jnp.concatenate([high, high], axis=1), forward[128:384, :]
         else:
-            high, low = split(block.reshape(count * 64, 128))
+            high, low = split(block.reshape(-1, 128))
             left, table = jnp.concatenate([high, low, high], axis=1), forward[...]
         yz = jnp.dot(left, table, preferred_element_type=F32)
         gx = jnp.stack(x_derivative([block[i] for i in range(8)], derivative))
         return gx, yz[:, :128].reshape(block.shape), yz[:, 128:].reshape(block.shape)
 
-    def state_terms(e):
-        rows = slice(8 * e, 8 * e + 8)
-        moved = jnp.stack(
-            [value[:, f * 32 + 8 * e : f * 32 + 8 * e + 8, :] for f in range(3)], axis=1
-        )
-        gx, gy, gz = gradients(moved, 3, True)
+    def state_terms(start):
+        rows = slice(start, start + 16)
+        moved = group(value, start, 16, 3)
+        gx, gy, gz = gradients(moved, True)
         shear = [gy[:, 0] + gx[:, 1], gz[:, 0] + gx[:, 2], gz[:, 1] + gy[:, 2]]
         normal = [gx[:, 0], gy[:, 1], gz[:, 2]]
         trace_sum = normal[0] + normal[1] + normal[2]
@@ -439,9 +446,9 @@
         state[6, :, rows, :] = lame_mu * mass * (intact * intact + residual_stiff)
         state[7, :, rows, :] = mass * (gc_inverse + 2.0 * driving)
 
-    def apply_transposed(e, block):
-        rows = slice(8 * e, 8 * e + 8)
-        gx, gy, gz = gradients(block, 4, False)
+    def apply_transposed(start, block):
+        rows = slice(start, start + 16)
+        gx, gy, gz = gradients(block, False)
         scaled = [state[n, :, rows, :] for n in range(6)]
         stiff = state[6, :, rows, :]
         vd = block[:, 3]
@@ -458,19 +465,19 @@
         along_x = jnp.stack([tensor[0], tensor[3], tensor[4], flux * gx[:, 3]], axis=1)
         along_y = jnp.stack([tensor[3], tensor[1], tensor[5], flux * gy[:, 3]], axis=1)
         along_z = jnp.stack([tensor[4], tensor[5], tensor[2], flux * gz[:, 3]], axis=1)
-        y_high, y_low = split(along_y.reshape(256, 128))
-        z_high, z_low = split(along_z.reshape(256, 128))
+        y_high, y_low = split(along_y.reshape(-1, 128))
+        z_high, z_low = split(along_z.reshape(-1, 128))
         one = jnp.dot(
             jnp.concatenate([y_high, z_high], axis=1), back[...], preferred_element_type=F32
         )
         two = jnp.dot(
             jnp.concatenate([y_low, z_low], axis=1), back[:, :128], preferred_element_type=F32
         )
-        total = (one[:, :128] + one[:, 128:] + two).reshape(8, 4, 8, 128)
+        total = (one[:, :128] + one[:, 128:] + two).reshape(block.shape)
         total = total + jnp.stack(x_derivative([along_x[i] for i in range(8)], derivative.T))
-        result = group(load, e) - total
+        result = group(load, start, 16) - total
         result = jnp.concatenate([result[:, :3], (result[:, 3] - nodal)[:, None]], axis=1)
-        put_group(summed, e, sum_z(result))
+        put_group(summed, start, 16, sum_z(result))
 
     def ship(r):
         messages = {}
@@ -485,31 +492,29 @@
 
     copies[1].wait()
     copies[2].wait()
-    for f in range(4):
-        put_tiles(to_tiles(adjoint_b[f]), summed, f * 32)
-    for e in range(4):
-        put_group(summed, e, sum_z(group(summed, e)))
+    put_tiles(to_tiles([adjoint_b[f] for f in range(4)]), [(summed, f * 32) for f in range(4)])
+    for start in (0, 16):
+        put_group(summed, start, 16, sum_z(group(summed, start, 16)))
     for e in range(3):
         sum_y(e)
     messages = ship(0)
 
     copies[3].wait()
-    for f in range(3):
-        put_tiles(to_tiles(displace_b[f]), value, f * 32)
     copies[4].wait()
     copies[5].wait()
-    put_tiles(to_tiles(damage_b[...]), keep.at[0], 0)
     copies[6].wait()
-    put_tiles(to_tiles(history_b[...]), keep.at[1], 0)
+    put_tiles(
+        to_tiles([displace_b[0], displace_b[1], displace_b[2], damage_b[...], history_b[...]]),
+        [(value, 0), (value, 32), (value, 64), (keep.at[0], 0), (keep.at[1], 0)],
+    )
     copies[7].wait()
     frozen = 1.0 - jnp.sum(chosen * frozen_b[...].astype(F32), axis=1, keepdims=True)
     low_half = lax.broadcasted_iota(jnp.int32, (32, 128), 1) < 64
     keep[2, 0] = jnp.where(low_half, frozen[:32], frozen[32:])
-    for e in range(4):
-        state_terms(e)
+    for start in (0, 16):
+        state_terms(start)
     copies[8].wait()
-    for f in range(4):
-        put_tiles(to_tiles(load_b[f]), load, f * 32)
+    put_tiles(to_tiles([load_b[f] for f in range(4)]), [(load, f * 32) for f in range(4)])
     copies[9].wait()
 
     def halved(condition, scalar):
@@ -518,30 +523,30 @@
     inv_z = halved(inner_z, 1.0) * halved(first_z & (sub > 0), 1.0) * halved(last_z & (sub < 7), 1.0)
     inv_z = inv_z * halved(first_z & (sub == 0), present[2][-1]) * halved(last_z & (sub == 7), present[2][1])
 
-    def average(e):
-        lower = 1.0 if e > 0 else present[1][-1]
-        upper = 1.0 if e < 3 else present[1][1]
-        scale = inv_z * halved(lane_j == 0, lower) * halved(lane_j == 7, upper)
+    def average(start):
+        planes = []
+        for t in (start // 8, start // 8 + 1):
+            lower = 1.0 if EY[t] > 0 else present[1][-1]
+            upper = 1.0 if EY[t] < 3 else present[1][1]
+            planes.append(inv_z * halved(lane_j == 0, lower) * halved(lane_j == 7, upper))
+        scale = jnp.concatenate(planes, axis=0)
         scales = [scale] * 8
         scales[0] = scale * (1.0 - 0.5 * present[0][-1])
         scales[7] = scale * (1.0 - 0.5 * present[0][1])
-        block = group(value, e) * jnp.stack(scales)[:, None]
-        put_group(kept, e, block)
+        block = group(value, start, 16) * jnp.stack(scales)[:, None]
+        put_group(kept, start, 16, block)
         return block
 
-    def relax(e):
-        return group(kept, e) + relaxation * group(value, e)
+    def relax(start):
+        return group(kept, start, 16) + relaxation * group(value, start, 16)
 
     for r, ready in ((0, average), (1, relax)):
         receive_early(r, messages)
         finish(messages)
-        early = [ready(e) for e in (1, 2)]
-        for e in (1, 2):
-            apply_transposed(e, early[e - 1])
+        apply_transposed(16, ready(16))
         sum_y(1)
         receive_late(r, messages)
-        for e in (0, 3):
-            apply_transposed(e, ready(e))
+        apply_transposed(0, ready(0))
         sum_y(0)
         sum_y(2)
         messages = ship(r + 1)
@@ -604,7 +609,7 @@
             pltpu.SemaphoreType.DMA((3, 26)),
         ],
         compiler_params=pltpu.CompilerParams(
-            collective_id=0, has_side_effects=True, vmem_limit_bytes=32 * 1024 * 1024
+            collective_id=0, has_side_effects=True, vmem_limit_bytes=56 * 1024 * 1024
         ),
     )(adjoint, load, displace, damage, history, frozen.reshape(1, 64), order, forward, back, swap)
 

time: 43.6 us -> 37.3 us (0.86)
  local copies, waits for them, and re-layouts: 8.7 us -> 1.87 us
  Pallas kernels: 34.5 us -> 35.3 us
    unnamed x21 -> x1, local copies, waits for them, and re-layouts: 8.7 us -> 1.87 us
    pallas_call x1, Pallas kernels: 34.5 us -> 35.3 us  [shards(): pl.pallas_call(kernel, out_shape=jax.ShapeDtypeStruct((4, 64, 512), F32),...]
where the time goes in v2:
time: 37.3 us; the launch traced here: 37.2 us
  Pallas kernels  35.3 us (95%)
  local copies, waits for them, and re-layouts  1.87 us (5%)
    pallas_call x1, Pallas kernels, shards(): pl.pallas_call(kernel, out_shape=jax.ShapeDtypeStruct((4, 64, 512), F32),...  35.3 us
    unnamed x1, local copies, waits for them, and re-layouts  1.87 us

profile of v2, /device:TPU:1, one launch (start us, length us, event | category | flops | bytes accessed | tf_op | source)
XLA Modules:
  0.0 37.2 jit_solution(17593187494459194414)
XLA Ops:
  0.0 35.3 %shard_map.100 = f32[4,64,512]{2,1,0:T(8,128)} custom-call(bf16[4,64,512]{2,1,0:T(8,128)(2,1)} %adjoint_h.1, bf16[4,64,512]{2,1,0:T(8,128)(2,1)} %load_h.1, bf16[3,64,512]{2,1,0:T(8,128)(2,1)} %displace_h.1, bf16[64,512]{1,0:T(8,128)(2,1)} %damage_h.1, bf16[64,512]{1,0:T(8,128)(2,1)} %history_h.1, s32[1,64]{1,0:T(1,128)} %bitcast.1, s32[1,64]{1,0:T(1,128)} %order_h.1, ...), custom_call_target="tpu_custom_call" | custom-call | tf_op jit(solution)/shard_map/pallas_call | solution.py:579
  35.3 1.9 %copy.12 = f32[4,64,512]{2,1,0:T(8,128)} copy(f32[4,64,512]{2,1,0:T(8,128)} %shard_map.100) | data formatting | bytes 1048576

commit v3 on v2

--- a/solution.py
+++ b/solution.py
@@ -28,8 +28,8 @@
     1.0,
 )
 
-EY = (0, 3, 1, 2)
-TILE = (0, 2, 3, 1)
+EY = ((3, 0), (1, 2))
+START = {ey: 64 * half + 8 * tile for half in range(2) for tile, ey in enumerate(EY[half])}
 
 DIRS = [
     (dx, dy, dz)
@@ -214,19 +214,32 @@
     def target(d):
         return tuple(along[axis][d[axis]] for axis in range(3))
 
+    has = [{-1: p > 0, 1: p < n - 1} for p, n in zip((px, py, pz), sizes)]
+    present = [{s: side[s].astype(F32) for s in (-1, 1)} for side in has]
+
+    def there(d):
+        sides = [has[axis][d[axis]] for axis in range(3) if d[axis] != 0]
+        found = sides[0]
+        for side in sides[1:]:
+            found = jnp.logical_and(found, side)
+        return found
+
+    to_there = {d: there(d) for d in DIRS}
+
+    def from_there(d):
+        return to_there[(-d[0], -d[1], -d[2])]
+
     barrier = pltpu.get_barrier_semaphore()
     for d in DIRS:
-        pl.semaphore_signal(barrier, inc=1, device_id=target(d), device_id_type=MESH)
+
+        @pl.when(to_there[d])
+        def _(d=d):
+            pl.semaphore_signal(barrier, inc=1, device_id=target(d), device_id_type=MESH)
+
+    around = [1 + side[-1].astype(jnp.int32) + side[1].astype(jnp.int32) for side in has]
+    neighbours = around[0] * around[1] * around[2] - 1
     for copy in copies[3:]:
         copy.start()
-
-    present = [
-        {
-            -1: (p > 0).astype(F32),
-            1: (p < n - 1).astype(F32),
-        }
-        for p, n in zip((px, py, pz), sizes)
-    ]
 
     lane = lax.broadcasted_iota(jnp.int32, (8, 128), 1)
     sub = lax.broadcasted_iota(jnp.int32, (8, 128), 0)
@@ -249,7 +262,7 @@
     copies[0].wait()
     row_id = lax.broadcasted_iota(jnp.int32, (64, 64), 0)
     tile_id = (row_id // 8) % 4
-    row_ey = jnp.where(tile_id == 1, 3, jnp.where(tile_id > 1, tile_id - 1, 0))
+    row_ey = (tile_id + 3) % 4
     place = row_ey * 16 + 2 * (row_id % 8) + row_id // 32
     chosen = fmask(place == order_b[...])
     pick = chosen.astype(BF16)
@@ -266,20 +279,25 @@
         )
         return tiles.reshape(len(fields) * 4, 32, 256)
 
-    def put_tiles(tiles, places):
-        for n, (ref, start) in enumerate(places):
+    def put_fields(tiles, ref, fields):
+        for f in range(fields):
             for a in range(4):
-                ref[2 * a, start : start + 32, :] = tiles[4 * n + a, :, :128]
-                ref[2 * a + 1, start : start + 32, :] = tiles[4 * n + a, :, 128:]
-
-    def group(ref, start, rows, fields=4):
-        return jnp.stack(
-            [ref[:, f * 32 + start : f * 32 + start + rows, :] for f in range(fields)], axis=1
-        )
-
-    def put_group(ref, start, rows, block):
-        for f in range(4):
-            ref[:, f * 32 + start : f * 32 + start + rows, :] = block[:, f]
+                for half in range(2):
+                    rows = slice(half * 64 + f * 16, half * 64 + f * 16 + 16)
+                    both = tiles[4 * f + a, half * 16 : half * 16 + 16, :]
+                    ref[2 * a, rows, :] = both[:, :128]
+                    ref[2 * a + 1, rows, :] = both[:, 128:]
+
+    def put_single(tiles, n):
+        for a in range(4):
+            keep[n, 2 * a] = tiles[a, :, :128]
+            keep[n, 2 * a + 1] = tiles[a, :, 128:]
+
+    def group(ref, half):
+        return ref[:, half * 64 : half * 64 + 64, :].reshape(8, 4, 16, 128)
+
+    def put_group(ref, half, block):
+        ref[:, half * 64 : half * 64 + 64, :] = block.reshape(8, 64, 128)
 
     def sum_z(block):
         flat = block.reshape(-1, 8, 128)
@@ -287,12 +305,32 @@
         total = flat + z_here * taken + z_next * pltpu.roll(taken, 1, 1)
         return total.reshape(block.shape)
 
-    def sum_y(e):
-        lower, upper = 8 * TILE[e], 8 * TILE[e + 1]
-        here, beyond = group(summed, lower, 8), group(summed, upper, 8)
-        taken = lane_swap(jnp.where(lane_j == 7, here, beyond), 56)
-        put_group(summed, lower, 8, here + j_end[1] * taken)
-        put_group(summed, upper, 8, beyond + j_end[-1] * taken)
+    def sum_y(e, spans=((0, 8),)):
+        for first, last in spans:
+            for f in range(4):
+                lower = slice(START[e] + f * 16, START[e] + f * 16 + 8)
+                upper = slice(START[e + 1] + f * 16, START[e + 1] + f * 16 + 8)
+                here, beyond = summed[first:last, lower, :], summed[first:last, upper, :]
+                taken = lane_swap(jnp.where(lane_j == 7, here, beyond), 56)
+                summed[first:last, lower, :] = here + j_end[1] * taken
+                summed[first:last, upper, :] = beyond + j_end[-1] * taken
+
+    def mask_of(half, tile, j):
+        return fmask((lane_k % 2 == half) & (sub % 2 == tile) & (lane_j == j))
+
+    inner_i = fmask(((lane_h == 1) | (lane_k > 1)) & ((lane_h == 0) | (lane_k < 6)))
+    packed_y = []
+    for ey in (0, 2):
+        half, tile = (START[ey] // 64, (START[ey] // 8) % 2)
+        half_up, tile_up = (START[ey + 1] // 64, (START[ey + 1] // 8) % 2)
+        packed_y.append((inner_i * mask_of(half, tile, 7), tile - tile_up, 56 + half - half_up))
+        packed_y.append((inner_i * mask_of(half_up, tile_up, 0), tile_up - tile, half_up - half - 56))
+
+    def packed_sum_y(face):
+        total = face
+        for wanted, tiles, lanes in packed_y:
+            total = total + wanted * lane_roll(pltpu.roll(face, tiles % 8, 0), lanes)
+        return total
 
     def pack_z(r):
         for n, (row, h, k) in enumerate(((0, 0, 0), (7, 1, 7))):
@@ -302,23 +340,25 @@
                 piece = summed[i, pl.ds(half * 64 + row, 8, stride=8), :]
                 moved = lane_roll(piece, (slot // 8 - h) * 64 + slot % 8 - k)
                 packed = jnp.where((lane_h == slot // 8) & (lane_k == slot % 8), moved, packed)
-            zs[r, n] = packed
+            zs[r, n] = packed_sum_y(packed)
 
     def pack_y(r):
-        for n, (t, j) in enumerate(((0, 0), (1, 7))):
+        for n, (ey, j) in enumerate(((0, 0), (3, 7))):
             for g in range(4):
                 packed = jnp.zeros((8, 128), F32)
                 for slot in range(8):
-                    row = (slot // 2) * 32 + 8 * t
+                    row = (slot // 2) * 16 + START[ey]
                     piece = summed[2 * g + slot % 2, row : row + 8, :]
                     packed = jnp.where(lane_j == slot, lane_roll(piece, 8 * (slot - j)), packed)
                 ys[r, n, g] = packed
 
-    def message(r, d):
+    def message(r, d, half=0):
         n = DIRS.index(d)
         dx, dy, dz = d
         if d in X_DIRS:
-            src, dst = summed.at[7 if dx > 0 else 0], xr.at[r, (dx + 1) // 2]
+            rows = pl.ds(64 * half, 64)
+            src, dst = summed.at[7 if dx > 0 else 0, rows], xr.at[r, (dx + 1) // 2, rows]
+            n = n if half == 0 else 26 + (dx + 1) // 2
         elif d in Y_DIRS:
             src, dst = ys.at[r, (dy + 1) // 2], yr.at[r, (dy + 1) // 2]
         elif d in XY_DIRS:
@@ -334,76 +374,91 @@
             device_id_type=MESH,
         )
 
-    def send(r, messages, dirs):
+    def send(r, dirs, half=0):
         for d in dirs:
-            messages[d] = message(r, d)
-            messages[d].start()
-
-    def finish(messages):
+            pl.when(to_there[d])(message(r, d, half).start)
+
+    def finish(r):
         for d in DIRS:
-            messages[d].wait_send()
-
-    def add_z(r, messages, dirs):
+            pl.when(to_there[d])(message(r, d).wait_send)
+        for d in X_DIRS:
+            pl.when(to_there[d])(message(r, d, 1).wait_send)
+
+    def arrive(r, dirs, half=0):
+        for d in dirs:
+            pl.when(from_there(d))(message(r, d, half).wait_recv)
+
+    def arrived(d, data):
+        return lax.select(from_there(d), data, jnp.zeros_like(data))
+
+    def z_faces(r, dirs):
+        arrive(r, dirs)
+        faces = []
         for dz in (-1, 1):
-            side = -dz
             face = None
             for d in dirs:
                 if d[2] != dz:
                     continue
-                messages[d].wait_recv()
-                part = zr[r, Z_DIRS.index(d)]
+                part = arrived(d, zr[r, Z_DIRS.index(d)])
                 dx, dy, _ = d
                 wanted = None
                 if dx != 0:
                     slots = (lane_k < 2) if dx > 0 else (lane_k >= 6)
-                    wanted = h_end[-dx] * fmask(slots) * present[0][-dx]
+                    wanted = h_end[-dx] * fmask(slots)
                 if dy != 0:
-                    mine = j_end[-dy] * fmask(sub % 4 == (0 if dy > 0 else 1)) * present[1][-dy]
+                    mine = mask_of(0, 1 if dy > 0 else 0, 0 if dy > 0 else 7)
                     wanted = mine if wanted is None else wanted * mine
-                    part = pltpu.roll(part, -dy % 8, 0)
+                    part = pltpu.roll(part, dy % 8, 0)
                 part = lane_roll(part, -70 * dx - 56 * dy)
                 if wanted is not None:
                     part = part * wanted
                 face = part if face is None else face + part
-            row, h, k = (0, 0, 0) if side < 0 else (7, 1, 7)
-            wanted = z_end[side] * present[2][side]
-            for slot in range(16):
-                i, half = slot // 2, slot % 2
+            faces.append(face)
+        return faces
+
+    def add_z(faces, half):
+        for dz, face in zip((-1, 1), faces):
+            row, h, k = (0, 0, 0) if dz > 0 else (7, 1, 7)
+            for i in range(8):
+                slot = 2 * i + half
                 where = pl.ds(half * 64 + row, 8, stride=8)
                 moved = lane_roll(face, (h - slot // 8) * 64 + k - slot % 8)
-                value[i, where, :] = value[i, where, :] + moved * wanted
-
-    def receive_early(r, messages):
+                value[i, where, :] = value[i, where, :] + moved * z_end[-dz]
+
+    def take_x(r, half):
+        rows = slice(64 * half, 64 * half + 64)
+        arrive(r, X_DIRS, half)
         for i in range(1, 7):
-            value[i] = summed[i]
+            value[i, rows, :] = summed[i, rows, :]
         for d in X_DIRS:
-            messages[d].wait_recv()
             i = 0 if d[0] > 0 else 7
-            value[i] = summed[i] + xr[r, (d[0] + 1) // 2] * present[0][-d[0]]
-        add_z(r, messages, Z_EARLY)
-
-    def receive_late(r, messages):
+            value[i, rows, :] = summed[i, rows, :] + arrived(d, xr[r, (d[0] + 1) // 2, rows, :])
+
+    def receive_early(r):
+        take_x(r, 1)
+        faces = z_faces(r, Z_EARLY)
+        add_z(faces, 1)
+        return faces
+
+    def receive_late(r, faces):
+        take_x(r, 0)
+        arrive(r, Y_DIRS + XY_DIRS)
         for d in Y_DIRS:
-            messages[d].wait_recv()
             dy = d[1]
-            side = -dy
-            faces = [yr[r, (dy + 1) // 2, g] for g in range(4)]
+            sides = [arrived(d, yr[r, (dy + 1) // 2, g]) for g in range(4)]
             for dx in (-1, 1):
                 e = (dx, dy, 0)
-                messages[e].wait_recv()
-                edge = lane_roll(xyr[r, XY_DIRS.index(e)], -8 * dx)
-                wanted = fmask(lane_j % 2 == (0 if dx > 0 else 1)) * present[0][-dx]
+                edge = lane_roll(arrived(e, xyr[r, XY_DIRS.index(e)]), -8 * dx)
                 g = 0 if dx > 0 else 3
-                faces[g] = faces[g] + edge * wanted
-            t, j = (0, 0) if side < 0 else (1, 7)
-            wanted = j_end[side] * present[1][side]
+                sides[g] = sides[g] + edge * fmask(lane_j % 2 == (0 if dx > 0 else 1))
+            ey, j = (0, 0) if dy > 0 else (3, 7)
             for i in range(8):
                 for f in range(4):
-                    slot = f * 2 + i % 2
-                    row = f * 32 + 8 * t
-                    moved = lane_roll(faces[i // 2], 8 * (j - slot))
-                    value[i, row : row + 8, :] = value[i, row : row + 8, :] + moved * wanted
-        add_z(r, messages, Z_LATE)
+                    row = f * 16 + START[ey]
+                    moved = lane_roll(sides[i // 2], 8 * (j - f * 2 - i % 2))
+                    value[i, row : row + 8, :] = value[i, row : row + 8, :] + moved * j_end[-dy]
+        late = z_faces(r, Z_LATE)
+        add_z([face + more for face, more in zip(faces, late)], 0)
 
     def brick():
         line_j = jnp.zeros((8, 128), F32)
@@ -425,9 +480,9 @@
         gx = jnp.stack(x_derivative([block[i] for i in range(8)], derivative))
         return gx, yz[:, :128].reshape(block.shape), yz[:, 128:].reshape(block.shape)
 
-    def state_terms(start):
-        rows = slice(start, start + 16)
-        moved = group(value, start, 16, 3)
+    def state_terms(half):
+        rows = slice(16 * half, 16 * half + 16)
+        moved = group(value, half)[:, :3]
         gx, gy, gz = gradients(moved, True)
         shear = [gy[:, 0] + gx[:, 1], gz[:, 0] + gx[:, 2], gz[:, 1] + gy[:, 2]]
         normal = [gx[:, 0], gy[:, 1], gz[:, 2]]
@@ -446,8 +501,8 @@
         state[6, :, rows, :] = lame_mu * mass * (intact * intact + residual_stiff)
         state[7, :, rows, :] = mass * (gc_inverse + 2.0 * driving)
 
-    def apply_transposed(start, block):
-        rows = slice(start, start + 16)
+    def apply_transposed(half, block):
+        rows = slice(16 * half, 16 * half + 16)
         gx, gy, gz = gradients(block, False)
         scaled = [state[n, :, rows, :] for n in range(6)]
         stiff = state[6, :, rows, :]
@@ -475,46 +530,48 @@
         )
         total = (one[:, :128] + one[:, 128:] + two).reshape(block.shape)
         total = total + jnp.stack(x_derivative([along_x[i] for i in range(8)], derivative.T))
-        result = group(load, start, 16) - total
+        result = group(load, half) - total
         result = jnp.concatenate([result[:, :3], (result[:, 3] - nodal)[:, None]], axis=1)
-        put_group(summed, start, 16, sum_z(result))
+        put_group(summed, half, sum_z(result))
 
     def ship(r):
-        messages = {}
+        for e in (0, 2):
+            sum_y(e, ((0, 1), (7, 8)))
         pack_z(r)
         if r == 0:
-            pl.semaphore_wait(barrier, len(DIRS))
-        send(r, messages, Z_ORDER)
-        send(r, messages, X_DIRS)
+            pl.semaphore_wait(barrier, neighbours)
+        send(r, X_DIRS, 1)
+        send(r, Z_ORDER)
+        send(r, X_DIRS, 0)
         pack_y(r)
-        send(r, messages, XY_DIRS + Y_DIRS)
-        return messages
+        send(r, XY_DIRS + Y_DIRS)
+        for e in (0, 2):
+            sum_y(e, ((1, 7),))
 
     copies[1].wait()
     copies[2].wait()
-    put_tiles(to_tiles([adjoint_b[f] for f in range(4)]), [(summed, f * 32) for f in range(4)])
-    for start in (0, 16):
-        put_group(summed, start, 16, sum_z(group(summed, start, 16)))
-    for e in range(3):
-        sum_y(e)
-    messages = ship(0)
+    put_fields(to_tiles([adjoint_b[f] for f in range(4)]), summed, 4)
+    for half in range(2):
+        put_group(summed, half, sum_z(group(summed, half)))
+    sum_y(1)
+    ship(0)
 
     copies[3].wait()
     copies[4].wait()
     copies[5].wait()
     copies[6].wait()
-    put_tiles(
-        to_tiles([displace_b[0], displace_b[1], displace_b[2], damage_b[...], history_b[...]]),
-        [(value, 0), (value, 32), (value, 64), (keep.at[0], 0), (keep.at[1], 0)],
-    )
+    tiles = to_tiles([displace_b[0], displace_b[1], displace_b[2], damage_b[...], history_b[...]])
+    put_fields(tiles, value, 3)
+    put_single(tiles[12:16], 0)
+    put_single(tiles[16:20], 1)
     copies[7].wait()
     frozen = 1.0 - jnp.sum(chosen * frozen_b[...].astype(F32), axis=1, keepdims=True)
     low_half = lax.broadcasted_iota(jnp.int32, (32, 128), 1) < 64
     keep[2, 0] = jnp.where(low_half, frozen[:32], frozen[32:])
-    for start in (0, 16):
-        state_terms(start)
+    for half in range(2):
+        state_terms(half)
     copies[8].wait()
-    put_tiles(to_tiles([load_b[f] for f in range(4)]), [(load, f * 32) for f in range(4)])
+    put_fields(to_tiles([load_b[f] for f in range(4)]), load, 4)
     copies[9].wait()
 
     def halved(condition, scalar):
@@ -523,42 +580,44 @@
     inv_z = halved(inner_z, 1.0) * halved(first_z & (sub > 0), 1.0) * halved(last_z & (sub < 7), 1.0)
     inv_z = inv_z * halved(first_z & (sub == 0), present[2][-1]) * halved(last_z & (sub == 7), present[2][1])
 
-    def average(start):
+    def average(half):
         planes = []
-        for t in (start // 8, start // 8 + 1):
-            lower = 1.0 if EY[t] > 0 else present[1][-1]
-            upper = 1.0 if EY[t] < 3 else present[1][1]
+        for ey in EY[half]:
+            lower = 1.0 if ey > 0 else present[1][-1]
+            upper = 1.0 if ey < 3 else present[1][1]
             planes.append(inv_z * halved(lane_j == 0, lower) * halved(lane_j == 7, upper))
         scale = jnp.concatenate(planes, axis=0)
         scales = [scale] * 8
         scales[0] = scale * (1.0 - 0.5 * present[0][-1])
         scales[7] = scale * (1.0 - 0.5 * present[0][1])
-        block = group(value, start, 16) * jnp.stack(scales)[:, None]
-        put_group(kept, start, 16, block)
+        block = group(value, half) * jnp.stack(scales)[:, None]
+        put_group(kept, half, block)
         return block
 
-    def relax(start):
-        return group(kept, start, 16) + relaxation * group(value, start, 16)
+    def relax(half):
+        return group(kept, half) + relaxation * group(value, half)
 
     for r, ready in ((0, average), (1, relax)):
-        receive_early(r, messages)
-        finish(messages)
-        apply_transposed(16, ready(16))
+        finish(r)
+        faces = receive_early(r)
+        apply_transposed(1, ready(1))
         sum_y(1)
-        receive_late(r, messages)
+        receive_late(r, faces)
         apply_transposed(0, ready(0))
-        sum_y(0)
-        sum_y(2)
-        messages = ship(r + 1)
-
-    receive_early(2, messages)
-    receive_late(2, messages)
+        ship(r + 1)
+
+    finish(2)
+    receive_late(2, receive_early(2))
     twice = jnp.concatenate([unpick, unpick], axis=1)
     for f in range(4):
-        rows = slice(f * 32, f * 32 + 32)
-        sides = jnp.stack(
-            [jnp.concatenate([value[2 * a, rows, :], value[2 * a + 1, rows, :]], axis=1) for a in range(4)]
-        )
+        sides = []
+        for a in range(4):
+            pair = []
+            for i in (2 * a, 2 * a + 1):
+                halves = [value[i, 64 * half + 16 * f : 64 * half + 16 * f + 16, :] for half in range(2)]
+                pair.append(jnp.concatenate(halves, axis=0))
+            sides.append(jnp.concatenate(pair, axis=1))
+        sides = jnp.stack(sides)
         high, low = split(sides.reshape(128, 256))
         both = jnp.concatenate([high, low], axis=0)
         moved = jnp.dot(both, swap[...], preferred_element_type=F32).astype(BF16)
@@ -570,7 +629,6 @@
             out_ref[f, :, a * 128 : a * 128 + 128] = jnp.dot(
                 twice, stacked, preferred_element_type=F32
             )
-    finish(messages)
 
 
 def shards(adjoint, load, displace, damage, history, frozen, order):
@@ -578,7 +636,7 @@
     hbm = pl.BlockSpec(memory_space=pltpu.HBM)
     return pl.pallas_call(
         kernel,
-        out_shape=jax.ShapeDtypeStruct((4, 64, 512), F32),
+        out_shape=pltpu.VMEM((4, 64, 512), F32),
         in_specs=[hbm] * 10,
         out_specs=pl.BlockSpec(memory_space=pltpu.VMEM),
         scratch_shapes=[
@@ -605,8 +663,8 @@
             pltpu.VMEM((3, 4, 8, 128), F32),
             pltpu.VMEM((3, 18, 8, 128), F32),
             pltpu.SemaphoreType.DMA((10,)),
-            pltpu.SemaphoreType.DMA((3, 26)),
-            pltpu.SemaphoreType.DMA((3, 26)),
+            pltpu.SemaphoreType.DMA((3, 28)),
+            pltpu.SemaphoreType.DMA((3, 28)),
         ],
         compiler_params=pltpu.CompilerParams(
             collective_id=0, has_side_effects=True, vmem_limit_bytes=56 * 1024 * 1024

time: 37.3 us -> 28.9 us (0.77)
  Pallas kernels: 35.3 us -> 28 us
  local copies, waits for them, and re-layouts: 1.87 us -> 0.8 us
    pallas_call x1, Pallas kernels: 35.3 us -> 28 us  [shards(): pl.pallas_call(kernel, out_shape=pltpu.VMEM((4, 64, 512), F32), in_specs=...]
    unnamed x1, local copies, waits for them, and re-layouts: 1.87 us -> 0.8 us
where the time goes in v3:
time: 28.9 us; the launch traced here: 28.8 us
  Pallas kernels  28 us (97%)
  local copies, waits for them, and re-layouts  0.8 us (3%)
    pallas_call x1, Pallas kernels, shards(): pl.pallas_call(kernel, out_shape=pltpu.VMEM((4, 64, 512), F32), in_specs=...  28 us
    unnamed x1, local copies, waits for them, and re-layouts  0.8 us

profile of v3, /device:TPU:1, one launch (start us, length us, event | category | flops | bytes accessed | tf_op | source)
XLA Modules:
  0.0 28.8 jit_solution(6697555756300160600)
XLA Ops:
  0.0 28.0 %shard_map.100 = f32[4,64,512]{2,1,0:T(8,128)S(1)} custom-call(bf16[4,64,512]{2,1,0:T(8,128)(2,1)} %adjoint_h.1, bf16[4,64,512]{2,1,0:T(8,128)(2,1)} %load_h.1, bf16[3,64,512]{2,1,0:T(8,128)(2,1)} %displace_h.1, bf16[64,512]{1,0:T(8,128)(2,1)} %damage_h.1, bf16[64,512]{1,0:T(8,128)(2,1)} %history_h.1, s32[1,64]{1,0:T(1,128)} %bitcast.1, s32[1,64]{1,0:T(1,128)} %order_h.1, ...), custom_call_target="tpu_custom_call" | custom-call | tf_op jit(solution)/shard_map/pallas_call | solution.py:637
  28.0 0.8 %copy.12 = f32[4,64,512]{2,1,0:T(8,128)} copy(f32[4,64,512]{2,1,0:T(8,128)S(1)} %shard_map.100) | data formatting | bytes 1048576

commit v4 on v3

--- a/solution.py
+++ b/solution.py
@@ -45,6 +45,7 @@
 Z_LATE = [d for d in Z_DIRS if d[1] != 0]
 Z_EARLY = [d for d in Z_DIRS if d[1] == 0]
 Z_ORDER = sorted(Z_DIRS, key=lambda d: -abs(d[0]) - abs(d[1]))
+GROUPS = (X_DIRS, X_DIRS, Y_DIRS, XY_DIRS, Z_EARLY, Z_LATE)
 
 
 def legendre_at(points, degree):
@@ -98,7 +99,7 @@
     f_high, f_low = split_np(np.concatenate([forward_y, forward_z], axis=1))
     forward = np.concatenate([f_high, f_high, f_low], axis=0)
     b_high, b_low = split_np(np.concatenate([back_y, back_z], axis=0))
-    back = np.concatenate([b_high, b_low], axis=1)
+    back = np.concatenate([b_high, b_high, b_low], axis=0)
     swap = np.zeros((2, 2, 64, 2, 2, 64))
     for h in range(2):
         for odd in range(2):
@@ -177,7 +178,9 @@
     xr,
     yr,
     xyr,
-    zr,
+    zer,
+    zlr,
+    zero,
     in_sem,
     send_sem,
     recv_sem,
@@ -266,7 +269,6 @@
     place = row_ey * 16 + 2 * (row_id % 8) + row_id // 32
     chosen = fmask(place == order_b[...])
     pick = chosen.astype(BF16)
-    unpick = chosen.T.astype(BF16)
 
     def to_tiles(fields):
         sides = []
@@ -299,11 +301,12 @@
     def put_group(ref, half, block):
         ref[:, half * 64 : half * 64 + 64, :] = block.reshape(8, 64, 128)
 
-    def sum_z(block):
-        flat = block.reshape(-1, 8, 128)
+    def sum_z(half, first, last):
+        rows = slice(64 * half, 64 * half + 64)
+        flat = summed[first:last, rows, :].reshape(-1, 8, 128)
         taken = lane_swap(jnp.where(first_z, pltpu.roll(flat, 7, 1), flat), 71)
         total = flat + z_here * taken + z_next * pltpu.roll(taken, 1, 1)
-        return total.reshape(block.shape)
+        summed[first:last, rows, :] = total.reshape(last - first, 64, 128)
 
     def sum_y(e, spans=((0, 8),)):
         for first, last in spans:
@@ -320,19 +323,24 @@
 
     inner_i = fmask(((lane_h == 1) | (lane_k > 1)) & ((lane_h == 0) | (lane_k < 6)))
     packed_y = []
-    for ey in (0, 2):
+    for ey in range(3):
         half, tile = (START[ey] // 64, (START[ey] // 8) % 2)
         half_up, tile_up = (START[ey + 1] // 64, (START[ey + 1] // 8) % 2)
-        packed_y.append((inner_i * mask_of(half, tile, 7), tile - tile_up, 56 + half - half_up))
-        packed_y.append((inner_i * mask_of(half_up, tile_up, 0), tile_up - tile, half_up - half - 56))
-
-    def packed_sum_y(face):
+        packed_y.append(
+            (
+                (inner_i * mask_of(half, tile, 7), tile - tile_up, 56 + half - half_up),
+                (inner_i * mask_of(half_up, tile_up, 0), tile_up - tile, half_up - half - 56),
+            )
+        )
+
+    def packed_sum_y(face, pairs):
         total = face
-        for wanted, tiles, lanes in packed_y:
-            total = total + wanted * lane_roll(pltpu.roll(face, tiles % 8, 0), lanes)
+        for e in pairs:
+            for wanted, tiles, lanes in packed_y[e]:
+                total = total + wanted * lane_roll(pltpu.roll(face, tiles % 8, 0), lanes)
         return total
 
-    def pack_z(r):
+    def pack_z(r, pairs):
         for n, (row, h, k) in enumerate(((0, 0, 0), (7, 1, 7))):
             packed = jnp.zeros((8, 128), F32)
             for slot in range(16):
@@ -340,7 +348,7 @@
                 piece = summed[i, pl.ds(half * 64 + row, 8, stride=8), :]
                 moved = lane_roll(piece, (slot // 8 - h) * 64 + slot % 8 - k)
                 packed = jnp.where((lane_h == slot // 8) & (lane_k == slot % 8), moved, packed)
-            zs[r, n] = packed_sum_y(packed)
+            zs[r, n] = packed_sum_y(packed, pairs)
 
     def pack_y(r):
         for n, (ey, j) in enumerate(((0, 0), (3, 7))):
@@ -350,61 +358,66 @@
                     row = (slot // 2) * 16 + START[ey]
                     piece = summed[2 * g + slot % 2, row : row + 8, :]
                     packed = jnp.where(lane_j == slot, lane_roll(piece, 8 * (slot - j)), packed)
-                ys[r, n, g] = packed
-
-    def message(r, d, half=0):
-        n = DIRS.index(d)
+                ys[r, n, 8 * g : 8 * g + 8] = packed
+
+    def slot_of(r, g, d):
+        n = GROUPS[g].index(d)
+        return (xr.at[r, 0], xr.at[r, 1], yr.at[r], xyr.at[r], zer.at[r], zlr.at[r])[g].at[n]
+
+    def message(r, g, d):
         dx, dy, dz = d
-        if d in X_DIRS:
-            rows = pl.ds(64 * half, 64)
-            src, dst = summed.at[7 if dx > 0 else 0, rows], xr.at[r, (dx + 1) // 2, rows]
-            n = n if half == 0 else 26 + (dx + 1) // 2
-        elif d in Y_DIRS:
-            src, dst = ys.at[r, (dy + 1) // 2], yr.at[r, (dy + 1) // 2]
-        elif d in XY_DIRS:
-            src, dst = ys.at[r, (dy + 1) // 2, 3 if dx > 0 else 0], xyr.at[r, XY_DIRS.index(d)]
+        if g < 2:
+            src = summed.at[7 if dx > 0 else 0, pl.ds(64 * g, 64)]
+        elif g == 2:
+            src = ys.at[r, (dy + 1) // 2]
+        elif g == 3:
+            src = ys.at[r, (dy + 1) // 2, pl.ds(24 if dx > 0 else 0, 8)]
         else:
-            src, dst = zs.at[r, (dz + 1) // 2], zr.at[r, Z_DIRS.index(d)]
+            src = zs.at[r, (dz + 1) // 2]
+        n = sum(len(dirs) for dirs in GROUPS[:g]) + GROUPS[g].index(d)
         return pltpu.make_async_remote_copy(
             src_ref=src,
-            dst_ref=dst,
+            dst_ref=slot_of(r, g, d),
             send_sem=send_sem.at[r, n],
-            recv_sem=recv_sem.at[r, n],
+            recv_sem=recv_sem.at[r, g],
             device_id=target(d),
             device_id_type=MESH,
         )
 
-    def send(r, dirs, half=0):
-        for d in dirs:
-            pl.when(to_there[d])(message(r, d, half).start)
+    def send(r, g, dirs=None):
+        for d in dirs or GROUPS[g]:
+            pl.when(to_there[d])(message(r, g, d).start)
+
+    def fill_absent(r):
+        for g in range(6):
+            source = zero if g < 2 else zero.at[pl.ds(0, 32)] if g == 2 else zero.at[pl.ds(0, 8)]
+            for d in GROUPS[g]:
+                slot = slot_of(r, g, d)
+                copy = pltpu.make_async_copy(source, slot, recv_sem.at[r, g])
+                pl.when(jnp.logical_not(from_there(d)))(copy.start)
 
     def finish(r):
-        for d in DIRS:
-            pl.when(to_there[d])(message(r, d).wait_send)
-        for d in X_DIRS:
-            pl.when(to_there[d])(message(r, d, 1).wait_send)
-
-    def arrive(r, dirs, half=0):
-        for d in dirs:
-            pl.when(from_there(d))(message(r, d, half).wait_recv)
-
-    def arrived(d, data):
-        return lax.select(from_there(d), data, jnp.zeros_like(data))
-
-    def z_faces(r, dirs):
-        arrive(r, dirs)
+        for g in range(6):
+            for d in GROUPS[g]:
+                pl.when(to_there[d])(message(r, g, d).wait_send)
+
+    def arrive(r, g):
+        slots = (xr.at[r, 0], xr.at[r, 1], yr.at[r], xyr.at[r], zer.at[r], zlr.at[r])[g]
+        pltpu.make_async_copy(slots, slots, recv_sem.at[r, g]).wait()
+
+    def z_faces(slots, dirs):
         faces = []
         for dz in (-1, 1):
             face = None
-            for d in dirs:
+            for n, d in enumerate(dirs):
                 if d[2] != dz:
                     continue
-                part = arrived(d, zr[r, Z_DIRS.index(d)])
+                part = slots[n]
                 dx, dy, _ = d
                 wanted = None
                 if dx != 0:
-                    slots = (lane_k < 2) if dx > 0 else (lane_k >= 6)
-                    wanted = h_end[-dx] * fmask(slots)
+                    near = (lane_k < 2) if dx > 0 else (lane_k >= 6)
+                    wanted = h_end[-dx] * fmask(near)
                 if dy != 0:
                     mine = mask_of(0, 1 if dy > 0 else 0, 0 if dy > 0 else 7)
                     wanted = mine if wanted is None else wanted * mine
@@ -427,28 +440,27 @@
 
     def take_x(r, half):
         rows = slice(64 * half, 64 * half + 64)
-        arrive(r, X_DIRS, half)
-        for i in range(1, 7):
-            value[i, rows, :] = summed[i, rows, :]
-        for d in X_DIRS:
+        arrive(r, half)
+        for n, d in enumerate(X_DIRS):
             i = 0 if d[0] > 0 else 7
-            value[i, rows, :] = summed[i, rows, :] + arrived(d, xr[r, (d[0] + 1) // 2, rows, :])
+            value[i, rows, :] = value[i, rows, :] + xr[r, half, n]
 
     def receive_early(r):
+        arrive(r, 4)
+        faces = z_faces(zer.at[r], Z_EARLY)
         take_x(r, 1)
-        faces = z_faces(r, Z_EARLY)
         add_z(faces, 1)
         return faces
 
     def receive_late(r, faces):
         take_x(r, 0)
-        arrive(r, Y_DIRS + XY_DIRS)
-        for d in Y_DIRS:
+        arrive(r, 2)
+        arrive(r, 3)
+        for n, d in enumerate(Y_DIRS):
             dy = d[1]
-            sides = [arrived(d, yr[r, (dy + 1) // 2, g]) for g in range(4)]
+            sides = [yr[r, n, 8 * g : 8 * g + 8] for g in range(4)]
             for dx in (-1, 1):
-                e = (dx, dy, 0)
-                edge = lane_roll(arrived(e, xyr[r, XY_DIRS.index(e)]), -8 * dx)
+                edge = lane_roll(xyr[r, XY_DIRS.index((dx, dy, 0))], -8 * dx)
                 g = 0 if dx > 0 else 3
                 sides[g] = sides[g] + edge * fmask(lane_j % 2 == (0 if dx > 0 else 1))
             ey, j = (0, 0) if dy > 0 else (3, 7)
@@ -457,7 +469,8 @@
                     row = f * 16 + START[ey]
                     moved = lane_roll(sides[i // 2], 8 * (j - f * 2 - i % 2))
                     value[i, row : row + 8, :] = value[i, row : row + 8, :] + moved * j_end[-dy]
-        late = z_faces(r, Z_LATE)
+        arrive(r, 5)
+        late = z_faces(zlr.at[r], Z_LATE)
         add_z([face + more for face, more in zip(faces, late)], 0)
 
     def brick():
@@ -482,7 +495,7 @@
 
     def state_terms(half):
         rows = slice(16 * half, 16 * half + 16)
-        moved = group(value, half)[:, :3]
+        moved = group(kept, half)[:, :3]
         gx, gy, gz = gradients(moved, True)
         shear = [gy[:, 0] + gx[:, 1], gz[:, 0] + gx[:, 2], gz[:, 1] + gy[:, 2]]
         normal = [gx[:, 0], gy[:, 1], gz[:, 2]]
@@ -522,46 +535,53 @@
         along_z = jnp.stack([tensor[4], tensor[5], tensor[2], flux * gz[:, 3]], axis=1)
         y_high, y_low = split(along_y.reshape(-1, 128))
         z_high, z_low = split(along_z.reshape(-1, 128))
-        one = jnp.dot(
-            jnp.concatenate([y_high, z_high], axis=1), back[...], preferred_element_type=F32
-        )
-        two = jnp.dot(
-            jnp.concatenate([y_low, z_low], axis=1), back[:, :128], preferred_element_type=F32
-        )
-        total = (one[:, :128] + one[:, 128:] + two).reshape(block.shape)
+        total = jnp.dot(
+            jnp.concatenate([y_high, z_high, y_low, z_low, y_high, z_high], axis=1),
+            back[...],
+            preferred_element_type=F32,
+        ).reshape(block.shape)
         total = total + jnp.stack(x_derivative([along_x[i] for i in range(8)], derivative.T))
         result = group(load, half) - total
         result = jnp.concatenate([result[:, :3], (result[:, 3] - nodal)[:, None]], axis=1)
-        put_group(summed, half, sum_z(result))
+        put_group(summed, half, result)
 
     def ship(r):
-        for e in (0, 2):
+        halves, pairs = ((0, 1), (0, 1, 2)) if r == 0 else ((0,), (0, 2))
+        for half in halves:
+            sum_z(half, 0, 1)
+            sum_z(half, 7, 8)
+        for e in pairs:
             sum_y(e, ((0, 1), (7, 8)))
-        pack_z(r)
+        pack_z(r, pairs)
         if r == 0:
             pl.semaphore_wait(barrier, neighbours)
-        send(r, X_DIRS, 1)
-        send(r, Z_ORDER)
-        send(r, X_DIRS, 0)
+        send(r, 1)
+        for d in Z_ORDER:
+            send(r, 4 if d in Z_EARLY else 5, [d])
+        send(r, 0)
+        for half in halves:
+            sum_z(half, 1, 7)
         pack_y(r)
-        send(r, XY_DIRS + Y_DIRS)
-        for e in (0, 2):
+        send(r, 3)
+        send(r, 2)
+        for e in pairs:
             sum_y(e, ((1, 7),))
+        value[...] = summed[...]
 
     copies[1].wait()
     copies[2].wait()
     put_fields(to_tiles([adjoint_b[f] for f in range(4)]), summed, 4)
-    for half in range(2):
-        put_group(summed, half, sum_z(group(summed, half)))
-    sum_y(1)
     ship(0)
+
+    zero[...] = jnp.zeros((64, 128), F32)
+    fill_absent(0)
 
     copies[3].wait()
     copies[4].wait()
     copies[5].wait()
     copies[6].wait()
     tiles = to_tiles([displace_b[0], displace_b[1], displace_b[2], damage_b[...], history_b[...]])
-    put_fields(tiles, value, 3)
+    put_fields(tiles, kept, 3)
     put_single(tiles[12:16], 0)
     put_single(tiles[16:20], 1)
     copies[7].wait()
@@ -597,38 +617,44 @@
     def relax(half):
         return group(kept, half) + relaxation * group(value, half)
 
+    fill_absent(1)
+    fill_absent(2)
+
     for r, ready in ((0, average), (1, relax)):
         finish(r)
         faces = receive_early(r)
         apply_transposed(1, ready(1))
+        sum_z(1, 0, 8)
         sum_y(1)
         receive_late(r, faces)
         apply_transposed(0, ready(0))
         ship(r + 1)
 
+    def emit(half):
+        block = value[:, 64 * half : 64 * half + 64, :].reshape(4, 2, 4, 16, 128)
+        sides = jnp.concatenate([block[:, 0], block[:, 1]], axis=3).reshape(256, 256)
+        high, low = split(sides)
+        moved = jnp.dot(
+            jnp.concatenate([high, low], axis=0), swap[...], preferred_element_type=F32
+        ).astype(BF16)
+        rows = jnp.concatenate([chosen[16 * half : 16 * half + 16], chosen[32 + 16 * half : 48 + 16 * half]], axis=0)
+        unpick = jnp.concatenate([rows, rows], axis=0).T.astype(BF16)
+        for f in range(4):
+            columns = []
+            for a in range(4):
+                parts = []
+                for n in (a * 64 + f * 16, 256 + a * 64 + f * 16):
+                    parts += [moved[n : n + 16, :128], moved[n : n + 16, 128:]]
+                columns.append(jnp.concatenate(parts, axis=0))
+            stacked = jnp.concatenate(columns, axis=1)
+            out = jnp.dot(unpick, stacked, preferred_element_type=F32)
+            out_ref[f] = out if half == 1 else out_ref[f] + out
+
     finish(2)
-    receive_late(2, receive_early(2))
-    twice = jnp.concatenate([unpick, unpick], axis=1)
-    for f in range(4):
-        sides = []
-        for a in range(4):
-            pair = []
-            for i in (2 * a, 2 * a + 1):
-                halves = [value[i, 64 * half + 16 * f : 64 * half + 16 * f + 16, :] for half in range(2)]
-                pair.append(jnp.concatenate(halves, axis=0))
-            sides.append(jnp.concatenate(pair, axis=1))
-        sides = jnp.stack(sides)
-        high, low = split(sides.reshape(128, 256))
-        both = jnp.concatenate([high, low], axis=0)
-        moved = jnp.dot(both, swap[...], preferred_element_type=F32).astype(BF16)
-        for a in range(4):
-            parts = []
-            for n in (a * 32, 128 + a * 32):
-                parts += [moved[n : n + 32, :128], moved[n : n + 32, 128:]]
-            stacked = jnp.concatenate(parts, axis=0)
-            out_ref[f, :, a * 128 : a * 128 + 128] = jnp.dot(
-                twice, stacked, preferred_element_type=F32
-            )
+    faces = receive_early(2)
+    emit(1)
+    receive_late(2, faces)
+    emit(0)
 
 
 def shards(adjoint, load, displace, damage, history, frozen, order):
@@ -648,7 +674,7 @@
             pltpu.VMEM((1, 64), jnp.int32),
             pltpu.VMEM((1, 64), jnp.int32),
             pltpu.VMEM((384, 256), BF16),
-            pltpu.VMEM((256, 256), BF16),
+            pltpu.VMEM((768, 128), BF16),
             pltpu.VMEM((256, 256), BF16),
             pltpu.VMEM((8, 128, 128), F32),
             pltpu.VMEM((8, 128, 128), F32),
@@ -656,15 +682,17 @@
             pltpu.VMEM((8, 128, 128), F32),
             pltpu.VMEM((8, 8, 32, 128), F32),
             pltpu.VMEM((3, 8, 32, 128), F32),
-            pltpu.VMEM((3, 2, 4, 8, 128), F32),
+            pltpu.VMEM((3, 2, 32, 128), F32),
             pltpu.VMEM((3, 2, 8, 128), F32),
-            pltpu.VMEM((3, 2, 128, 128), F32),
-            pltpu.VMEM((3, 2, 4, 8, 128), F32),
+            pltpu.VMEM((3, 2, 2, 64, 128), F32),
+            pltpu.VMEM((3, 2, 32, 128), F32),
             pltpu.VMEM((3, 4, 8, 128), F32),
-            pltpu.VMEM((3, 18, 8, 128), F32),
+            pltpu.VMEM((3, 6, 8, 128), F32),
+            pltpu.VMEM((3, 12, 8, 128), F32),
+            pltpu.VMEM((64, 128), F32),
             pltpu.SemaphoreType.DMA((10,)),
             pltpu.SemaphoreType.DMA((3, 28)),
-            pltpu.SemaphoreType.DMA((3, 28)),
+            pltpu.SemaphoreType.DMA((3, 6)),
         ],
         compiler_params=pltpu.CompilerParams(
             collective_id=0, has_side_effects=True, vmem_limit_bytes=56 * 1024 * 1024

time: 28.9 us -> 28.1 us (0.972)
  Pallas kernels: 28 us -> 27.2 us
    pallas_call x1, Pallas kernels: 28 us -> 27.2 us  [shards(): pl.pallas_call(kernel, out_shape=pltpu.VMEM((4, 64, 512), F32), in_specs=...]
where the time goes in v4:
time: 28.1 us; the launch traced here: 28 us
  Pallas kernels  27.2 us (97%)
  local copies, waits for them, and re-layouts  0.8 us (3%)
    pallas_call x1, Pallas kernels, shards(): pl.pallas_call(kernel, out_shape=pltpu.VMEM((4, 64, 512), F32), in_specs=...  27.2 us
    unnamed x1, local copies, waits for them, and re-layouts  0.8 us

profile of v4, /device:TPU:1, one launch (start us, length us, event | category | flops | bytes accessed | tf_op | source)
XLA Modules:
  0.0 28.0 jit_solution(12983815418919313504)
XLA Ops:
  0.0 27.2 %shard_map.100 = f32[4,64,512]{2,1,0:T(8,128)S(1)} custom-call(bf16[4,64,512]{2,1,0:T(8,128)(2,1)} %adjoint_h.1, bf16[4,64,512]{2,1,0:T(8,128)(2,1)} %load_h.1, bf16[3,64,512]{2,1,0:T(8,128)(2,1)} %displace_h.1, bf16[64,512]{1,0:T(8,128)(2,1)} %damage_h.1, bf16[64,512]{1,0:T(8,128)(2,1)} %history_h.1, s32[1,64]{1,0:T(1,128)} %bitcast.1, s32[1,64]{1,0:T(1,128)} %order_h.1, ...), custom_call_target="tpu_custom_call" | custom-call | tf_op jit(solution)/shard_map/pallas_call | solution.py:663
  27.2 0.8 %copy.12 = f32[4,64,512]{2,1,0:T(8,128)} copy(f32[4,64,512]{2,1,0:T(8,128)S(1)} %shard_map.100) | data formatting | bytes 1048576

commit v5 on v4

--- a/solution.py
+++ b/solution.py
@@ -99,7 +99,7 @@
     f_high, f_low = split_np(np.concatenate([forward_y, forward_z], axis=1))
     forward = np.concatenate([f_high, f_high, f_low], axis=0)
     b_high, b_low = split_np(np.concatenate([back_y, back_z], axis=0))
-    back = np.concatenate([b_high, b_high, b_low], axis=0)
+    back = np.concatenate([b_high, b_low], axis=1)
     swap = np.zeros((2, 2, 64, 2, 2, 64))
     for h in range(2):
         for odd in range(2):
@@ -233,7 +233,7 @@
         return to_there[(-d[0], -d[1], -d[2])]
 
     barrier = pltpu.get_barrier_semaphore()
-    for d in DIRS:
+    for d in sorted(DIRS, key=lambda d: -abs(d[0]) - abs(d[1]) - abs(d[2])):
 
         @pl.when(to_there[d])
         def _(d=d):
@@ -308,7 +308,7 @@
         total = flat + z_here * taken + z_next * pltpu.roll(taken, 1, 1)
         summed[first:last, rows, :] = total.reshape(last - first, 64, 128)
 
-    def sum_y(e, spans=((0, 8),)):
+    def sum_y(e, spans):
         for first, last in spans:
             for f in range(4):
                 lower = slice(START[e] + f * 16, START[e] + f * 16 + 8)
@@ -326,21 +326,18 @@
     for ey in range(3):
         half, tile = (START[ey] // 64, (START[ey] // 8) % 2)
         half_up, tile_up = (START[ey + 1] // 64, (START[ey + 1] // 8) % 2)
-        packed_y.append(
-            (
-                (inner_i * mask_of(half, tile, 7), tile - tile_up, 56 + half - half_up),
-                (inner_i * mask_of(half_up, tile_up, 0), tile_up - tile, half_up - half - 56),
-            )
-        )
-
-    def packed_sum_y(face, pairs):
+        packed_y += [
+            (inner_i * mask_of(half, tile, 7), tile - tile_up, 56 + half - half_up),
+            (inner_i * mask_of(half_up, tile_up, 0), tile_up - tile, half_up - half - 56),
+        ]
+
+    def packed_sum_y(face):
         total = face
-        for e in pairs:
-            for wanted, tiles, lanes in packed_y[e]:
-                total = total + wanted * lane_roll(pltpu.roll(face, tiles % 8, 0), lanes)
+        for wanted, tiles, lanes in packed_y:
+            total = total + wanted * lane_roll(pltpu.roll(face, tiles % 8, 0), lanes)
         return total
 
-    def pack_z(r, pairs):
+    def pack_z(r):
         for n, (row, h, k) in enumerate(((0, 0, 0), (7, 1, 7))):
             packed = jnp.zeros((8, 128), F32)
             for slot in range(16):
@@ -348,7 +345,7 @@
                 piece = summed[i, pl.ds(half * 64 + row, 8, stride=8), :]
                 moved = lane_roll(piece, (slot // 8 - h) * 64 + slot % 8 - k)
                 packed = jnp.where((lane_h == slot // 8) & (lane_k == slot % 8), moved, packed)
-            zs[r, n] = packed_sum_y(packed, pairs)
+            zs[r, n] = packed_sum_y(packed)
 
     def pack_y(r):
         for n, (ey, j) in enumerate(((0, 0), (3, 7))):
@@ -514,8 +511,8 @@
         state[6, :, rows, :] = lame_mu * mass * (intact * intact + residual_stiff)
         state[7, :, rows, :] = mass * (gc_inverse + 2.0 * driving)
 
-    def apply_transposed(half, block):
-        rows = slice(16 * half, 16 * half + 16)
+    def apply_tile(half, tile, block):
+        rows = slice(16 * half + 8 * tile, 16 * half + 8 * tile + 8)
         gx, gy, gz = gradients(block, False)
         scaled = [state[n, :, rows, :] for n in range(6)]
         stiff = state[6, :, rows, :]
@@ -535,36 +532,40 @@
         along_z = jnp.stack([tensor[4], tensor[5], tensor[2], flux * gz[:, 3]], axis=1)
         y_high, y_low = split(along_y.reshape(-1, 128))
         z_high, z_low = split(along_z.reshape(-1, 128))
-        total = jnp.dot(
-            jnp.concatenate([y_high, z_high, y_low, z_low, y_high, z_high], axis=1),
-            back[...],
-            preferred_element_type=F32,
-        ).reshape(block.shape)
+        one = jnp.dot(
+            jnp.concatenate([y_high, z_high], axis=1), back[...], preferred_element_type=F32
+        )
+        two = jnp.dot(
+            jnp.concatenate([y_low, z_low], axis=1), back[:, :128], preferred_element_type=F32
+        )
+        total = (one[:, :128] + one[:, 128:] + two).reshape(block.shape)
         total = total + jnp.stack(x_derivative([along_x[i] for i in range(8)], derivative.T))
-        result = group(load, half) - total
-        result = jnp.concatenate([result[:, :3], (result[:, 3] - nodal)[:, None]], axis=1)
-        put_group(summed, half, result)
+        result = group(load, half)[:, :, 8 * tile : 8 * tile + 8] - total
+        return jnp.concatenate([result[:, :3], (result[:, 3] - nodal)[:, None]], axis=1)
+
+    def apply_transposed(half, block):
+        parts = [apply_tile(half, n, block[:, :, 8 * n : 8 * n + 8]) for n in range(2)]
+        put_group(summed, half, jnp.concatenate(parts, axis=2))
 
     def ship(r):
-        halves, pairs = ((0, 1), (0, 1, 2)) if r == 0 else ((0,), (0, 2))
-        for half in halves:
+        for half in range(2):
             sum_z(half, 0, 1)
             sum_z(half, 7, 8)
-        for e in pairs:
+        for e in range(3):
             sum_y(e, ((0, 1), (7, 8)))
-        pack_z(r, pairs)
+        pack_z(r)
         if r == 0:
             pl.semaphore_wait(barrier, neighbours)
         send(r, 1)
         for d in Z_ORDER:
             send(r, 4 if d in Z_EARLY else 5, [d])
         send(r, 0)
-        for half in halves:
+        for half in range(2):
             sum_z(half, 1, 7)
         pack_y(r)
         send(r, 3)
         send(r, 2)
-        for e in pairs:
+        for e in range(3):
             sum_y(e, ((1, 7),))
         value[...] = summed[...]
 
@@ -624,8 +625,6 @@
         finish(r)
         faces = receive_early(r)
         apply_transposed(1, ready(1))
-        sum_z(1, 0, 8)
-        sum_y(1)
         receive_late(r, faces)
         apply_transposed(0, ready(0))
         ship(r + 1)
@@ -674,7 +673,7 @@
             pltpu.VMEM((1, 64), jnp.int32),
             pltpu.VMEM((1, 64), jnp.int32),
             pltpu.VMEM((384, 256), BF16),
-            pltpu.VMEM((768, 128), BF16),
+            pltpu.VMEM((256, 256), BF16),
             pltpu.VMEM((256, 256), BF16),
             pltpu.VMEM((8, 128, 128), F32),
             pltpu.VMEM((8, 128, 128), F32),

time: 28.1 us -> 28.1 us (level)
  no operation moved by 1% of the time
where the time goes in v5:
time: 28.1 us; the launch traced here: 28 us
  Pallas kernels  27.2 us (97%)
  local copies, waits for them, and re-layouts  0.8 us (3%)
    pallas_call x1, Pallas kernels, shards(): pl.pallas_call(kernel, out_shape=pltpu.VMEM((4, 64, 512), F32), in_specs=...  27.2 us
    unnamed x1, local copies, waits for them, and re-layouts  0.8 us

profile of v5, /device:TPU:1, one launch (start us, length us, event | category | flops | bytes accessed | tf_op | source)
XLA Modules:
  0.0 28.0 jit_solution(4711619204016265650)
XLA Ops:
  0.0 27.2 %shard_map.100 = f32[4,64,512]{2,1,0:T(8,128)S(1)} custom-call(bf16[4,64,512]{2,1,0:T(8,128)(2,1)} %adjoint_h.1, bf16[4,64,512]{2,1,0:T(8,128)(2,1)} %load_h.1, bf16[3,64,512]{2,1,0:T(8,128)(2,1)} %displace_h.1, bf16[64,512]{1,0:T(8,128)(2,1)} %damage_h.1, bf16[64,512]{1,0:T(8,128)(2,1)} %history_h.1, s32[1,64]{1,0:T(1,128)} %bitcast.1, s32[1,64]{1,0:T(1,128)} %order_h.1, ...), custom_call_target="tpu_custom_call" | custom-call | tf_op jit(solution)/shard_map/pallas_call | solution.py:662
  27.2 0.8 %copy.12 = f32[4,64,512]{2,1,0:T(8,128)} copy(f32[4,64,512]{2,1,0:T(8,128)S(1)} %shard_map.100) | data formatting | bytes 1048576

commit v6 on v5

--- a/solution.py
+++ b/solution.py
@@ -321,14 +321,13 @@
     def mask_of(half, tile, j):
         return fmask((lane_k % 2 == half) & (sub % 2 == tile) & (lane_j == j))
 
-    inner_i = fmask(((lane_h == 1) | (lane_k > 1)) & ((lane_h == 0) | (lane_k < 6)))
     packed_y = []
     for ey in range(3):
         half, tile = (START[ey] // 64, (START[ey] // 8) % 2)
         half_up, tile_up = (START[ey + 1] // 64, (START[ey + 1] // 8) % 2)
         packed_y += [
-            (inner_i * mask_of(half, tile, 7), tile - tile_up, 56 + half - half_up),
-            (inner_i * mask_of(half_up, tile_up, 0), tile_up - tile, half_up - half - 56),
+            (mask_of(half, tile, 7), tile - tile_up, 56 + half - half_up),
+            (mask_of(half_up, tile_up, 0), tile_up - tile, half_up - half - 56),
         ]
 
     def packed_sum_y(face):
@@ -548,23 +547,25 @@
         put_group(summed, half, jnp.concatenate(parts, axis=2))
 
     def ship(r):
+        pack_z(r)
         for half in range(2):
             sum_z(half, 0, 1)
             sum_z(half, 7, 8)
         for e in range(3):
             sum_y(e, ((0, 1), (7, 8)))
-        pack_z(r)
         if r == 0:
             pl.semaphore_wait(barrier, neighbours)
+        for d in Z_ORDER[:8]:
+            send(r, 5, [d])
         send(r, 1)
-        for d in Z_ORDER:
+        for d in Z_ORDER[8:]:
             send(r, 4 if d in Z_EARLY else 5, [d])
-        send(r, 0)
         for half in range(2):
             sum_z(half, 1, 7)
         pack_y(r)
         send(r, 3)
         send(r, 2)
+        send(r, 0)
         for e in range(3):
             sum_y(e, ((1, 7),))
         value[...] = summed[...]

time: 28.1 us -> 27.4 us (0.975)
  Pallas kernels: 27.2 us -> 26.6 us
    pallas_call x1, Pallas kernels: 27.2 us -> 26.6 us  [shards(): pl.pallas_call(kernel, out_shape=pltpu.VMEM((4, 64, 512), F32), in_specs=...]
where the time goes in v6:
time: 27.4 us
  Pallas kernels  26.6 us (97%)
  local copies, waits for them, and re-layouts  0.8 us (3%)
    pallas_call x1, Pallas kernels, shards(): pl.pallas_call(kernel, out_shape=pltpu.VMEM((4, 64, 512), F32), in_specs=...  26.6 us
    unnamed x1, local copies, waits for them, and re-layouts  0.8 us

profile of v6, /device:TPU:1, one launch (start us, length us, event | category | flops | bytes accessed | tf_op | source)
XLA Modules:
  0.0 27.4 jit_solution(4736308005550318279)
XLA Ops:
  0.0 26.6 %shard_map.100 = f32[4,64,512]{2,1,0:T(8,128)S(1)} custom-call(bf16[4,64,512]{2,1,0:T(8,128)(2,1)} %adjoint_h.1, bf16[4,64,512]{2,1,0:T(8,128)(2,1)} %load_h.1, bf16[3,64,512]{2,1,0:T(8,128)(2,1)} %displace_h.1, bf16[64,512]{1,0:T(8,128)(2,1)} %damage_h.1, bf16[64,512]{1,0:T(8,128)(2,1)} %history_h.1, s32[1,64]{1,0:T(1,128)} %bitcast.1, s32[1,64]{1,0:T(1,128)} %order_h.1, ...), custom_call_target="tpu_custom_call" | custom-call | tf_op jit(solution)/shard_map/pallas_call | solution.py:663
  26.6 0.8 %copy.12 = f32[4,64,512]{2,1,0:T(8,128)} copy(f32[4,64,512]{2,1,0:T(8,128)S(1)} %shard_map.100) | data formatting | bytes 1048576

commit v7 on v6

--- a/solution.py
+++ b/solution.py
@@ -436,7 +436,6 @@
 
     def take_x(r, half):
         rows = slice(64 * half, 64 * half + 64)
-        arrive(r, half)
         for n, d in enumerate(X_DIRS):
             i = 0 if d[0] > 0 else 7
             value[i, rows, :] = value[i, rows, :] + xr[r, half, n]
@@ -444,14 +443,13 @@
     def receive_early(r):
         arrive(r, 4)
         faces = z_faces(zer.at[r], Z_EARLY)
+        arrive(r, 1)
         take_x(r, 1)
         add_z(faces, 1)
         return faces
 
     def receive_late(r, faces):
         take_x(r, 0)
-        arrive(r, 2)
-        arrive(r, 3)
         for n, d in enumerate(Y_DIRS):
             dy = d[1]
             sides = [yr[r, n, 8 * g : 8 * g + 8] for g in range(4)]
@@ -465,7 +463,6 @@
                     row = f * 16 + START[ey]
                     moved = lane_roll(sides[i // 2], 8 * (j - f * 2 - i % 2))
                     value[i, row : row + 8, :] = value[i, row : row + 8, :] + moved * j_end[-dy]
-        arrive(r, 5)
         late = z_faces(zlr.at[r], Z_LATE)
         add_z([face + more for face, more in zip(faces, late)], 0)
 
@@ -510,7 +507,7 @@
         state[6, :, rows, :] = lame_mu * mass * (intact * intact + residual_stiff)
         state[7, :, rows, :] = mass * (gc_inverse + 2.0 * driving)
 
-    def apply_tile(half, tile, block):
+    def forward_tile(half, tile, block):
         rows = slice(16 * half + 8 * tile, 16 * half + 8 * tile + 8)
         gx, gy, gz = gradients(block, False)
         scaled = [state[n, :, rows, :] for n in range(6)]
@@ -531,19 +528,26 @@
         along_z = jnp.stack([tensor[4], tensor[5], tensor[2], flux * gz[:, 3]], axis=1)
         y_high, y_low = split(along_y.reshape(-1, 128))
         z_high, z_low = split(along_z.reshape(-1, 128))
+        return along_x, (y_high, y_low, z_high, z_low), nodal
+
+    def backward_tile(half, tile, pieces):
+        along_x, (y_high, y_low, z_high, z_low), nodal = pieces
         one = jnp.dot(
             jnp.concatenate([y_high, z_high], axis=1), back[...], preferred_element_type=F32
         )
         two = jnp.dot(
             jnp.concatenate([y_low, z_low], axis=1), back[:, :128], preferred_element_type=F32
         )
-        total = (one[:, :128] + one[:, 128:] + two).reshape(block.shape)
+        total = (one[:, :128] + one[:, 128:] + two).reshape(along_x.shape)
         total = total + jnp.stack(x_derivative([along_x[i] for i in range(8)], derivative.T))
         result = group(load, half)[:, :, 8 * tile : 8 * tile + 8] - total
         return jnp.concatenate([result[:, :3], (result[:, 3] - nodal)[:, None]], axis=1)
 
-    def apply_transposed(half, block):
-        parts = [apply_tile(half, n, block[:, :, 8 * n : 8 * n + 8]) for n in range(2)]
+    def forward_half(half, block):
+        return [forward_tile(half, n, block[:, :, 8 * n : 8 * n + 8]) for n in range(2)]
+
+    def backward_half(half, pieces):
+        parts = [backward_tile(half, n, pieces[n]) for n in range(2)]
         put_group(summed, half, jnp.concatenate(parts, axis=2))
 
     def ship(r):
@@ -625,9 +629,12 @@
     for r, ready in ((0, average), (1, relax)):
         finish(r)
         faces = receive_early(r)
-        apply_transposed(1, ready(1))
+        pieces = forward_half(1, ready(1))
+        for g in (0, 2, 3, 5):
+            arrive(r, g)
         receive_late(r, faces)
-        apply_transposed(0, ready(0))
+        backward_half(1, pieces)
+        backward_half(0, forward_half(0, ready(0)))
         ship(r + 1)
 
     def emit(half):
@@ -653,6 +660,8 @@
     finish(2)
     faces = receive_early(2)
     emit(1)
+    for g in (0, 2, 3, 5):
+        arrive(2, g)
     receive_late(2, faces)
     emit(0)
 

time: 27.4 us -> 26.3 us (0.960)
  Pallas kernels: 26.6 us -> 25.4 us
    pallas_call x1, Pallas kernels: 26.6 us -> 25.4 us  [shards(): pl.pallas_call(kernel, out_shape=pltpu.VMEM((4, 64, 512), F32), in_specs=...]
where the time goes in v7:
time: 26.3 us; the launch traced here: 26.2 us
  Pallas kernels  25.4 us (97%)
  local copies, waits for them, and re-layouts  0.8 us (3%)
    pallas_call x1, Pallas kernels, shards(): pl.pallas_call(kernel, out_shape=pltpu.VMEM((4, 64, 512), F32), in_specs=...  25.4 us
    unnamed x1, local copies, waits for them, and re-layouts  0.8 us

profile of v7, /device:TPU:1, one launch (start us, length us, event | category | flops | bytes accessed | tf_op | source)
XLA Modules:
  0.0 26.2 jit_solution(866375672828822586)
XLA Ops:
  0.0 25.4 %shard_map.100 = f32[4,64,512]{2,1,0:T(8,128)S(1)} custom-call(bf16[4,64,512]{2,1,0:T(8,128)(2,1)} %adjoint_h.1, bf16[4,64,512]{2,1,0:T(8,128)(2,1)} %load_h.1, bf16[3,64,512]{2,1,0:T(8,128)(2,1)} %displace_h.1, bf16[64,512]{1,0:T(8,128)(2,1)} %damage_h.1, bf16[64,512]{1,0:T(8,128)(2,1)} %history_h.1, s32[1,64]{1,0:T(1,128)} %bitcast.1, s32[1,64]{1,0:T(1,128)} %order_h.1, ...), custom_call_target="tpu_custom_call" | custom-call | tf_op jit(solution)/shard_map/pallas_call | solution.py:672
  25.4 0.8 %copy.12 = f32[4,64,512]{2,1,0:T(8,128)} copy(f32[4,64,512]{2,1,0:T(8,128)S(1)} %shard_map.100) | data formatting | bytes 1048576

commit v8 on v7

--- a/solution.py
+++ b/solution.py
@@ -552,15 +552,15 @@
 
     def ship(r):
         pack_z(r)
-        for half in range(2):
-            sum_z(half, 0, 1)
-            sum_z(half, 7, 8)
-        for e in range(3):
-            sum_y(e, ((0, 1), (7, 8)))
         if r == 0:
             pl.semaphore_wait(barrier, neighbours)
         for d in Z_ORDER[:8]:
             send(r, 5, [d])
+        for half in range(2):
+            sum_z(half, 0, 1)
+            sum_z(half, 7, 8)
+        for e in (0, 2, 1):
+            sum_y(e, ((0, 1), (7, 8)))
         send(r, 1)
         for d in Z_ORDER[8:]:
             send(r, 4 if d in Z_EARLY else 5, [d])
@@ -570,7 +570,7 @@
         send(r, 3)
         send(r, 2)
         send(r, 0)
-        for e in range(3):
+        for e in (0, 2, 1):
             sum_y(e, ((1, 7),))
         value[...] = summed[...]
 

time: 26.3 us -> 26.4 us (level)
  no operation moved by 1% of the time
where the time goes in v8:
time: 26.4 us
  Pallas kernels  25.5 us (97%)
  local copies, waits for them, and re-layouts  0.8 us (3%)
    pallas_call x1, Pallas kernels, shards(): pl.pallas_call(kernel, out_shape=pltpu.VMEM((4, 64, 512), F32), in_specs=...  25.5 us
    unnamed x1, local copies, waits for them, and re-layouts  0.8 us

profile of v8, /device:TPU:1, one launch (start us, length us, event | category | flops | bytes accessed | tf_op | source)
XLA Modules:
  0.0 26.4 jit_solution(5870474649657871589)
XLA Ops:
  0.0 25.5 %shard_map.100 = f32[4,64,512]{2,1,0:T(8,128)S(1)} custom-call(bf16[4,64,512]{2,1,0:T(8,128)(2,1)} %adjoint_h.1, bf16[4,64,512]{2,1,0:T(8,128)(2,1)} %load_h.1, bf16[3,64,512]{2,1,0:T(8,128)(2,1)} %displace_h.1, bf16[64,512]{1,0:T(8,128)(2,1)} %damage_h.1, bf16[64,512]{1,0:T(8,128)(2,1)} %history_h.1, s32[1,64]{1,0:T(1,128)} %bitcast.1, s32[1,64]{1,0:T(1,128)} %order_h.1, ...), custom_call_target="tpu_custom_call" | custom-call | tf_op jit(solution)/shard_map/pallas_call | solution.py:672
  25.6 0.8 %copy.12 = f32[4,64,512]{2,1,0:T(8,128)} copy(f32[4,64,512]{2,1,0:T(8,128)S(1)} %shard_map.100) | data formatting | bytes 1048576
